TPU v7x, 128 devices: a whole 4x4x4 slice. The times are simulated.
128 devices in a mesh: seq: 16 (over z, x), tp: 2 (over core), dp: 4 (over y).
Axes of the slice: x: 4, y: 4, z: 4, core: 2. Of those that a mesh axis runs over, the one named last changes fastest.
Arguments:
- media_tokens: bfloat16 [4, 8192, 1408], P('dp', 'seq'), as said below
- latents: bfloat16 [1024, 1408], replicated, as said below
- query_weight: bfloat16 [1408, 1408], P(None, 'tp'), as said below
- key_weight: bfloat16 [1408, 1408], P(None, 'tp'), as said below
- value_weight: bfloat16 [1408, 1408], P(None, 'tp'), may hold values from -0.15625 to 0.15625
- out_weight: bfloat16 [1408, 1408], P('tp'), may hold values from -0.15625 to 0.15625
- cotangent: bfloat16 [4, 1024, 1408], P('dp'), may hold values from -6 to 6
Outputs:
- resampled: bfloat16 [4, 1024, 1408], P('dp', None, 'tp')
- grad_latents: float32 [1024, 1408], P('seq', ('tp', 'dp'))
- grad_query: float32 [1408, 1408], P(('seq', 'dp'), 'tp')
- grad_key: float32 [1408, 1408], P(('seq', 'dp'), 'tp')
- grad_value: float32 [1408, 1408], P(('seq', 'dp'), 'tp')
- grad_out: float32 [1408, 1408], P('tp', ('seq', 'dp'))
Inputs may be any that keep to these rules, and one draw needn't show every extreme that they name: `media_tokens`: video features of order one. `latents`: latent entries of order one. `query_weight`: entries of order 1408^-0.5. `key_weight`: entries of order 1408^-0.5.
All inputs are finite; a program needn't handle non-finite values.
Results may differ from a plain program's by a relative error of at most 0.034.
The roundings to bfloat16 on the way count: a program that leaves them out, or rounds other values in their place, can miss the bound.
Values sent between devices are 32-bit elements; how exact they have to be, the bound alone decides.
No kernel may reach another device: no remote copies, remote signals or barrier semaphores. Data moves between devices by JAX's collectives and lax.ppermute only.
A program may use at most 192 MiB of HBM per device.

v0:
```python
import functools

import jax
import jax.numpy as jnp
from jax import lax
from jax.experimental import pallas as pl
from jax.experimental.pallas import tpu as pltpu
from jax.sharding import PartitionSpec as P

HD = 88
VMEM = 56 * 1024 * 1024
F32 = jnp.float32
BF16 = jnp.bfloat16
NT = (((1,), (1,)), ((), ()))
TN = (((0,), (0,)), ((), ()))


def params():
    return pltpu.CompilerParams(vmem_limit_bytes=VMEM)


def cost(flops, size):
    return pl.CostEstimate(flops=int(flops), bytes_accessed=int(size), transcendentals=0)


def dot(a, b, dims=(((1,), (0,)), ((), ()))):
    return lax.dot_general(a, b, dims, preferred_element_type=F32)


def layer_norm(rows):
    average = jnp.mean(rows, -1, keepdims=True)
    centered = rows - average
    variance = jnp.mean(centered * centered, -1, keepdims=True)
    inv_std = lax.rsqrt(variance + 1e-05)
    return (centered * inv_std, inv_std)


def norm_backward(normed, inv_std, upstream):
    mean_up = jnp.mean(upstream, -1, keepdims=True)
    mean_cross = jnp.mean(upstream * normed, -1, keepdims=True)
    return inv_std * (upstream - mean_up - normed * mean_cross)


def project_kernel(media, kw, vw, latents, qw, cot, ow, mn, ln, k, v, q, u, *scratch):
    arrays = [media, kw, vw, latents, qw, cot, ow, mn, ln, k, v, q, u]
    held, (arrive, leave) = scratch[: len(arrays)], scratch[len(arrays) :]
    media_at, kw_at, vw_at, latents_at, qw_at, cot_at, ow_at, mn_at, ln_at, k_at, v_at, q_at, u_at = held
    fetch = [pltpu.make_async_copy(arrays[i], held[i], arrive.at[i]) for i in range(7)]
    store = [pltpu.make_async_copy(held[7 + i], arrays[7 + i], leave.at[i]) for i in range(6)]
    for copy in fetch:
        copy.start()

    def chunks(count, body):
        size = min(256, count)

        @pl.loop(0, count // size)
        def _(i):
            body(pl.ds(pl.multiple_of(i * size, size), size))

    def normalise(source, target):
        def body(rows):
            target[:, rows] = layer_norm(source[rows, :].astype(F32))[0].T.astype(BF16)

        chunks(source.shape[0], body)

    def split(target, cols, value):
        for head in range(target.shape[0]):
            target[head, :, cols] = value[head * HD : (head + 1) * HD, :].astype(BF16)

    fetch[0].wait()
    normalise(media_at, mn_at)
    store[0].start()
    for i, weight, target in ((1, kw_at, k_at), (2, vw_at, v_at)):
        fetch[i].wait()
        chunks(
            mn_at.shape[1],
            lambda cols: split(target, cols, dot(weight[...], mn_at[:, cols])),
        )
        store[1 + i].start()
    fetch[3].wait()
    normalise(latents_at, ln_at)
    store[1].start()
    fetch[4].wait()
    chunks(
        ln_at.shape[1],
        lambda cols: split(q_at, cols, dot(qw_at[...], ln_at[:, cols]) * HD ** (-0.5)),
    )
    store[4].start()
    fetch[5].wait()
    fetch[6].wait()
    chunks(
        cot_at.shape[0],
        lambda rows: split(u_at, rows, dot(ow_at[...], cot_at[rows, :], NT)),
    )
    store[5].start()
    for copy in store:
        copy.wait()


def project(media, latents, cot, qw, kw, vw, ow):
    tokens, width = media.shape
    count = latents.shape[0]
    inner = qw.shape[0]
    heads = inner // HD
    ins = (media, kw, vw, latents, qw, cot, ow)
    outs = [
        jax.ShapeDtypeStruct(size, BF16)
        for size in (
            (width, tokens), (width, count),
            (heads, HD, tokens), (heads, HD, tokens), (heads, HD, count), (heads, HD, count),
        )
    ]
    anywhere = pl.BlockSpec(memory_space=pl.ANY)
    return pl.pallas_call(
        project_kernel,
        in_specs=[anywhere] * len(ins),
        out_specs=[anywhere] * len(outs),
        out_shape=outs,
        scratch_shapes=[pltpu.VMEM(a.shape, BF16) for a in (*ins, *outs)]
        + [pltpu.SemaphoreType.DMA((len(ins),)), pltpu.SemaphoreType.DMA((len(outs),))],
        compiler_params=params(),
        cost_estimate=cost(4 * (tokens + count) * width * inner, 24e6),
        name="project",
    )(*ins)


def forward_kernel(chunk, q_ref, k_ref, v_ref, u_ref, w_ref, stat_ref):
    step = pl.program_id(0)
    group, _, count = q_ref.shape
    half = count // 2

    def attend(item, keys, start, side, inner, limit):
        head = step * group + item
        cols = pl.ds(start, chunk)
        scores = dot(keys, q_ref[item, :, cols])
        top = jnp.max(scores, 0, keepdims=True) if limit is None else limit
        weights = jnp.exp(scores - top)
        weighted = dot(v_ref[item], weights.astype(BF16))
        w_ref[side, item, :, pl.ds(inner, chunk)] = weighted
        stat_ref[0, pl.ds(head, 1), cols] = top
        stat_ref[1, pl.ds(head, 1), cols] = jnp.sum(weights, 0, keepdims=True)
        stat_ref[2, pl.ds(head, 1), cols] = jnp.sum(
            u_ref[item, :, cols].astype(F32) * weighted, 0, keepdims=True
        )

    limits = []
    for item in range(group):
        q, k = q_ref[item].astype(F32), k_ref[item].astype(F32)
        longest = jnp.max(jnp.sum(k * k, 0, keepdims=True), 1, keepdims=True)
        limits.append(jnp.sqrt(jnp.sum(q * q, 0, keepdims=True) * longest) * 1.0001)
    highest = functools.reduce(jnp.maximum, [jnp.max(limit) for limit in limits])

    @pl.when(highest < 32.0)
    def _():
        for item in range(group):
            keys = k_ref[item].astype(F32).T.astype(BF16)
            for start in range(0, count, chunk):
                limit = limits[item][:, start : start + chunk]
                attend(item, keys, start, start // half, start % half, limit)

    @pl.when(jnp.logical_not(highest < 32.0))
    def _():
        per_side = half // chunk

        @pl.loop(0, group * 2 * per_side)
        def _(turn):
            item, side, place = turn // (2 * per_side), turn // per_side % 2, turn % per_side
            inner = pl.multiple_of(place * chunk, chunk)
            start = pl.multiple_of(side * half + inner, chunk)
            keys = k_ref[item].astype(F32).T.astype(BF16)
            attend(item, keys, start, side, inner, None)


def forward(q, k, v, u):
    heads, _, count = q.shape
    tokens = k.shape[2]
    group = 2
    per_head = lambda n: pl.BlockSpec((group, HD, n), lambda h: (h, 0, 0))
    return pl.pallas_call(
        functools.partial(forward_kernel, min(256, count // 2)),
        grid=(heads // group,),
        in_specs=[per_head(count), per_head(tokens), per_head(tokens), per_head(count)],
        out_specs=[
            pl.BlockSpec((2, group, HD, count // 2), lambda h: (0, h, 0, 0)),
            pl.BlockSpec((3, heads, count), lambda h: (0, 0, 0)),
        ],
        out_shape=[
            jax.ShapeDtypeStruct((2, heads, HD, count // 2), F32),
            jax.ShapeDtypeStruct((3, heads, count), F32),
        ],
        compiler_params=params(),
        cost_estimate=cost(16 * heads * count * tokens * HD, 9e6),
        name="attend",
    )(q, k, v, u)


def backward_kernel(
    chunk, q_ref, k_ref, v_ref, u_ref, stat_ref, dq_ref, dkv_ref, done_ref
):
    group, _, count = q_ref.shape
    half = count // 2
    for item in range(group):
        head = pl.program_id(0) * group + item
        keys_t = k_ref[item]
        keys = keys_t.astype(F32).T.astype(BF16)
        vals = v_ref[item].astype(F32).T.astype(BF16)
        key_grad = jnp.zeros(keys.shape, F32)
        value_grad = jnp.zeros(vals.shape, F32)
        total = stat_ref[1, pl.ds(head, 1), :]
        lse = stat_ref[0, pl.ds(head, 1), :] + jnp.log(total)
        delta = stat_ref[2, pl.ds(head, 1), :] / total
        for start in range(0, count, chunk):
            cols = slice(start, start + chunk)
            q = q_ref[item, :, cols]
            u = u_ref[item, :, cols]
            probs = jnp.exp(dot(keys, q) - lse[:, cols])
            grad = (probs * (dot(vals, u) - delta[:, cols])).astype(BF16)
            value_grad += dot(probs.astype(BF16), u.astype(F32).T.astype(BF16))
            key_grad += dot(grad, q.astype(F32).T.astype(BF16))
            side, inner = divmod(start, half)
            dq_ref[side, item, :, inner : inner + chunk] = dot(keys_t, grad)
        dkv_ref[0, item] = key_grad.T.astype(BF16)
        dkv_ref[1, item] = value_grad.T.astype(BF16)
    done_ref[...] = jnp.zeros_like(done_ref)


def backward(q, k, v, u, stats):
    heads, _, count = q.shape
    tokens = k.shape[2]
    group = 1
    per_head = lambda n: pl.BlockSpec((group, HD, n), lambda h: (h, 0, 0))
    return pl.pallas_call(
        functools.partial(backward_kernel, min(256, count // 2)),
        grid=(heads // group,),
        in_specs=[
            per_head(count), per_head(tokens), per_head(tokens), per_head(count),
            pl.BlockSpec((3, heads, count), lambda h: (0, 0, 0)),
        ],
        out_specs=[
            pl.BlockSpec((2, group, HD, count // 2), lambda h: (0, h, 0, 0)),
            pl.BlockSpec((2, group, HD, tokens), lambda h: (0, h, 0, 0)),
            pl.BlockSpec((8, 128), lambda h: (0, 0)),
        ],
        out_shape=[
            jax.ShapeDtypeStruct((2, heads, HD, count // 2), F32),
            jax.ShapeDtypeStruct((2, heads, HD, tokens), BF16),
            jax.ShapeDtypeStruct((8, 128), F32),
        ],
        compiler_params=params(),
        cost_estimate=cost(40 * heads * count * tokens * HD, 9e6),
        name="attend_back",
    )(q, k, v, u, stats)


def sum_kernel(pieces_ref, *refs):
    refs[-1][...] = jnp.sum(pieces_ref[...], 0)


def sum_pieces(pieces, *after):
    return pl.pallas_call(
        sum_kernel,
        in_specs=[pl.BlockSpec(memory_space=pltpu.VMEM)] + [pl.BlockSpec(memory_space=pl.ANY)] * len(after),
        out_shape=jax.ShapeDtypeStruct(pieces.shape[1:], F32),
        compiler_params=params(),
        cost_estimate=cost(pieces.size, 4 * pieces.size),
        name="sum_pieces",
    )(pieces, *after)


def out_kernel(att_ref, rows_ref, own_ref, other_ref, after_ref, grad_ref, keep_ref, send_ref):
    att = att_ref[0].reshape(own_ref.shape[1], att_ref.shape[3]).astype(BF16)
    term = dot(rows_ref[...], att, NT)

    @pl.when(pl.program_id(0) == 0)
    def _():
        grad_ref[...] = term

    @pl.when(pl.program_id(0) > 0)
    def _():
        grad_ref[...] += term

    send_ref[...] = dot(other_ref[...], att)
    keep_ref[...] = dot(own_ref[...], att)


def out_step(att, rows, own, other, after):
    _, heads, _, half = att.shape
    width, inner = own.shape
    share = rows.shape[0]
    whole = lambda a: pl.BlockSpec(a.shape, lambda i: (0, 0))
    return pl.pallas_call(
        out_kernel,
        grid=(2,),
        in_specs=[
            pl.BlockSpec((1, heads, HD, half), lambda i: (i, 0, 0, 0)),
            pl.BlockSpec((share, half), lambda i: (0, i)),
            whole(own),
            whole(other),
            pl.BlockSpec(memory_space=pl.ANY),
        ],
        out_specs=[
            pl.BlockSpec((share, inner), lambda i: (0, 0)),
            pl.BlockSpec((width, half), lambda i: (0, i)),
            pl.BlockSpec((width, half), lambda i: (0, i)),
        ],
        out_shape=[
            jax.ShapeDtypeStruct((share, inner), F32),
            jax.ShapeDtypeStruct((width, 2 * half), F32),
            jax.ShapeDtypeStruct((width, 2 * half), F32),
        ],
        compiler_params=params(),
        cost_estimate=cost(8 * half * inner * width, 12e6),
        name="project_out",
    )(att, rows, own, other, after)


def query_kernel(pieces_ref, norm_ref, out_ref):
    places, share, _ = out_ref.shape
    heads = places // 2
    total = jnp.sum(pieces_ref[...], 0)
    depth, half = total.shape
    rows = half // heads
    proj = (total * HD ** (-0.5)).astype(BF16)
    term = dot(norm_ref[...], proj, NT)
    for place in range(places):
        strip = place % heads * rows
        out_ref[place, :, :depth] = term[place * share : (place + 1) * share, :]
        out_ref[place, :depth, 128 : 128 + rows] = total[:, strip : strip + rows]


def query_step(pieces, norm, places):
    _, depth, half = pieces.shape
    width = norm.shape[0]
    return pl.pallas_call(
        query_kernel,
        out_shape=jax.ShapeDtypeStruct((places, width // places, 256), F32),
        compiler_params=params(),
        cost_estimate=cost(2 * half * width * depth, 6e6),
        name="query_grad",
    )(pieces, norm)


def latent_kernel(pieces_ref, qw_ref, latents_ref, cot_ref, out_ref):
    heads, depth, rows = pieces_ref.shape
    proj = pieces_ref[...].reshape(heads * depth, rows) * HD ** (-0.5)
    up = dot(proj.T.astype(BF16), qw_ref[...])
    hat, inv = layer_norm(latents_ref[...].astype(F32))
    term = norm_backward(hat, inv, up) + cot_ref[...].astype(F32) / 2
    size = out_ref.shape[2]
    for block in range(out_ref.shape[0]):
        out_ref[block] = term[:, block * size : (block + 1) * size]


def latent_step(pieces, qw, latents, cot, blocks):
    rows, width = latents.shape
    return pl.pallas_call(
        latent_kernel,
        out_shape=jax.ShapeDtypeStruct((blocks, rows, width // blocks), F32),
        compiler_params=params(),
        cost_estimate=cost(2 * rows * qw.size, 4e6),
        name="latent_grad",
    )(pieces, qw, latents, cot)


def shift(value, axis, by, side=None, minor=True):
    size = lax.axis_size(axis)
    if side is None:
        pairs = [(i, (i + by) % size) for i in range(size)]
    elif minor:
        pairs = [(i, i // side * side + (i % side + by) % side) for i in range(size)]
    else:
        pairs = [(i, (i + by * side) % size) for i in range(size)]
    return lax.ppermute(value, axis, pairs)


def pick(blocks, index):
    return lax.dynamic_index_in_dim(blocks, index, 0, False)


def scatter_sum(blocks, axis, place, side=None, minor=True):
    size = blocks.shape[0]
    total = pick(blocks, place)
    for by in range(1, size):
        total = total + shift(pick(blocks, (place + by) % size), axis, by, side, minor)
    return total


def relay_start(blocks, place, cut, send):
    far = pick(blocks, (place + 2) % 4)
    return send(far[:cut], 1), send(far[cut:], -1)


def relay_end(blocks, place, cut, send, front, back):
    ahead = pick(blocks, (place + 1) % 4)
    behind = pick(blocks, (place + 3) % 4)
    ahead = jnp.concatenate([ahead[:cut] + front, ahead[cut:]], 0)
    behind = jnp.concatenate([behind[:cut], behind[cut:] + back], 0)
    return pick(blocks, place) + send(ahead, 1) + send(behind, -1)


def merge_stats(stats, side, minor):
    parts = [stats] + [shift(stats, "seq", by, side, minor) for by in range(1, side)]
    top = functools.reduce(jnp.maximum, [p[0] for p in parts])
    factors = [jnp.exp(p[0] - top) for p in parts]
    total = sum(p[1] * f for p, f in zip(parts, factors))
    delta = sum(p[2] * f for p, f in zip(parts, factors))
    return jnp.stack([top, total, delta])


def local(media_tokens, latents, query_weight, key_weight, value_weight, out_weight, cotangent):
    inner = query_weight.shape[1]
    width = query_weight.shape[0]
    heads = inner // HD
    count = latents.shape[0]
    half = count // 2
    seq, tp, dp = (lax.axis_index(a) for a in ("seq", "tp", "dp"))
    seqs, tps, dps = (lax.axis_size(a) for a in ("seq", "tp", "dp"))
    side = 4
    share = width // seqs
    part = share // dps
    padded = -(-part // 8) * 8
    rows = count // seqs
    upstream = cotangent[0]
    query_turned = query_weight.T

    media_norm, latent_norm, k, v, q, u = project(
        media_tokens[0], latents, upstream, query_turned, key_weight.T, value_weight.T, out_weight
    )
    weighted, stats = forward(q, k, v, u)

    whole = merge_stats(merge_stats(stats, side, True), side, False)
    factor = (jnp.exp(stats[0] - whole[0]) / whole[1]).reshape(heads, 2, 1, half).transpose(1, 0, 2, 3)

    scaled = (weighted * factor).reshape(seqs, HD, half)
    attended_pieces = lax.all_to_all(scaled, "seq", 0, 0, tiled=True)
    dq, dkv, done = backward(q, k, v, u, whole)
    seq, tp, done = lax.optimization_barrier((seq, tp, done))

    query_pieces = lax.all_to_all(dq.reshape(seqs, HD, half), "seq", 0, 0, tiled=True)

    major, minor = seq // side, seq % side
    blocks = media_norm.reshape(seqs, dps, part, -1).transpose(1, 0, 2, 3)
    blocks = jnp.pad(blocks, ((0, 0), (0, 0), (0, padded - part), (0, 0)))
    blocks = blocks.reshape(dps * seqs * padded, -1)
    grads = dkv.reshape(2 * inner, -1)
    split = (inner // 128 + 1) * 128
    terms = [dot(blocks, grads[:split], NT), dot(blocks, grads[split:], NT)]
    terms = [t.reshape(dps, seqs * padded, -1) for t in terms]
    ring = (dp, seqs * padded // 2, lambda value, by: shift(value, "dp", by))
    halves = [relay_start(t, *ring) for t in terms]
    attended = sum_pieces(attended_pieces, terms[1], *halves[0])
    terms = [relay_end(t, *ring, *h) for t, h in zip(terms, halves)]
    first, second = (t.reshape(side, side, padded, -1) for t in terms)
    first = scatter_sum(first.transpose(1, 0, 2, 3), "seq", minor, side, True)
    first = scatter_sum(first, "seq", major, side, False)
    second = scatter_sum(second, "seq", major, side, False)
    second = scatter_sum(second, "seq", minor, side, True)
    grad_key = first[:part, :inner]
    grad_value = jnp.concatenate([first[:part, inner:], second[:part]], 1)

    side_of = seq // heads
    norm_half = lax.dynamic_slice_in_dim(latent_norm, side_of * half, half, 1)
    term = query_step(query_pieces, norm_half, seqs)
    sent = lax.all_to_all(term, "seq", 0, 0, tiled=True)
    strips = lax.dynamic_slice(sent, (side_of * heads, 0, 128), (heads, HD, rows))
    latent_rows = lax.dynamic_slice_in_dim(latents, seq * rows, rows, 0)
    cot_rows = lax.dynamic_slice_in_dim(upstream, seq * rows, rows, 0)
    back = latent_step(strips, query_turned, latent_rows, cot_rows, tps * dps)
    blocks = (sent[:heads, :, :HD] + sent[heads:, :, :HD]).transpose(1, 0, 2)
    grad_query = scatter_sum(blocks.reshape(dps, part, inner), "dp", dp)
    grad_latents = jnp.sum(lax.all_to_all(back, ("tp", "dp"), 0, 0, tiled=True), 0)

    attended = lax.all_gather(attended, "seq")
    cot_cols = lax.dynamic_slice_in_dim(upstream, seq * share, share, 1).T
    own = lax.dynamic_slice_in_dim(out_weight, tp * inner, inner, 1).T
    other = lax.dynamic_slice_in_dim(out_weight, (1 - tp) * inner, inner, 1).T
    latent_cols = lax.dynamic_slice_in_dim(latents, tp * inner, inner, 1).T
    out_rows, keep, away = out_step(
        attended.reshape(2, heads, HD, half), cot_cols, own, other, sent
    )
    arrived = lax.ppermute(away, "tp", [(0, 1), (1, 0)])
    resampled = (latent_cols.astype(F32) + (keep + arrived)).astype(BF16).T[None]
    grad_out = scatter_sum(out_rows.reshape(dps, part, inner), "dp", dp).T

    return (resampled, grad_latents, grad_query, grad_key, grad_value, grad_out)


def solution(mesh):
    placed = (
        P("dp", "seq", None),
        P(),
        P(None, "tp"),
        P(None, "tp"),
        P(None, "tp"),
        P("tp", None),
        P("dp", None, None),
    )
    return jax.shard_map(
        local,
        mesh=mesh,
        in_specs=placed,
        out_specs=(
            P("dp", None, "tp"),
            P("seq", ("tp", "dp")),
            P(("seq", "dp"), "tp"),
            P(("seq", "dp"), "tp"),
            P(("seq", "dp"), "tp"),
            P("tp", ("seq", "dp")),
        ),
        check_vma=False,
    )
```

profile of v0, /device:TPU:0, one launch (start us, length us, event | category | flops | bytes accessed | tf_op | source)
XLA Modules:
  0.0 296.4 jit_solution(14479025757478427156)
XLA Ops:
  7.2 14.9 %project.1 = (bf16[1408,512]{1,0:T(8,128)(2,1)}, bf16[1408,1024]{1,0:T(8,128)(2,1)}, bf16[8,88,512]{2,1,0:T(8,128)(2,1)}, bf16[8,88,512]{2,1,0:T(8,128)(2,1)}, b...) custom-call(bf16[512,1408]{1,0:T(8,128)(2,1)} %bitcast.205, bf16[704,1408]{1,0:T(8,128)(2,1)} %bitcast.203, ...), custom_call_target="tpu_custom_call" | custom-call | flops 6090129408 | bytes 24000000 | tf_op jit(solution)/shard_map/project/pallas_call | solution.py:114
  22.1 22.1 %attend.1 = (f32[2,8,88,512]{3,2,1,0:T(8,128)}, f32[3,8,1024]{2,1,0:T(8,128)}) custom-call(bf16[8,88,1024]{2,1,0:T(8,128)(2,1)} %get-tuple-element.22.q_ref, bf16[8,88,512]{2,1,0:T(8,128)(2,1)} %get-tuple-element.23.k_ref, bf16[8,88,512]{2,1,0:T(8,128)(2,1)} %get-tuple-element.24.v_ref, bf16[8,88,1024]{2,1,0:T(8,128)(2,1)} %get-tuple-element.25.u_ref), custom_call_target="tpu_custom_call" | custom-call | flops 5905580032 | bytes 9000000 | tf_op jit(solution)/shard_map/attend/pallas_call | solution.py:179
  56.8 4.1 %collective-permute-start.5 = (f32[3,8,1024]{2,1,0:T(8,128)S(1)}, f32[3,8,1024]{2,1,0:T(8,128)S(1)}, u32[]{:S(2)}, u32[]{:S(2)}) collective-permute-start(f32[3,8,1024]{2,1,0:T(8,128)S(1)} %pad_maximum_fusion.4), channel_id=1, source_target_pairs={{0,96},{8,104},{16,112},{24,120},{32,0},{40,8},{48,16},{56,24},{64... | collective-permute-start | bytes 294920 | tf_op jit(solution)/shard_map/ppermute | solution.py:373
  68.2 3.9 %broadcast_multiply_fusion = f32[2,8,88,512]{3,2,1,0:T(8,128)} fusion(f32[2,8,88,512]{3,2,1,0:T(8,128)} %get-tuple-element.26, f32[2,8,512]{2,1,0:T(8,128)S(1)} %divide_bitcast_fusion), kind=kLoop, calls=%fused_computation.3 | loop fusion | flops 720896 | bytes 5799936 | tf_op jit(solution)/shard_map/mul | solution.py:434
  72.1 3.7 %all-to-all-start = ((f32[16,88,512]{2,1,0:T(8,128)}), f32[16,88,512]{2,1,0:T(8,128)S(1)}, u32[]{:S(2)}, u32[]{:S(2)}) async-start(f32[16,88,512]{2,1,0:T(8,128)} %bitcast.22), calls=%async_computation | async-start | bytes 5767168 | tf_op jit(solution)/shard_map/all_to_all | solution.py:435
  75.9 3.3 %reshape.333 = bf16[16,4,22,512]{3,2,1,0:T(8,128)(2,1)} reshape(bf16[1408,512]{1,0:T(8,128)(2,1)} %get-tuple-element.28) | data formatting | bytes 2883584 | tf_op jit(solution)/shard_map/reshape | solution.py:442
  84.2 15.4 %attend_back.1 = (f32[2,8,88,512]{3,2,1,0:T(8,128)}, bf16[2,8,88,512]{3,2,1,0:T(8,128)(2,1)}, f32[8,128]{1,0:T(8,128)}) custom-call(bf16[8,88,1024]{2,1,0:T(8,128)(2,1)} %get-tuple-element.22.q_ref, bf16[8,88,512]{2,1,0:T(8,128)(2,1)} %get-tuple-element.23.k_ref, bf16[8,88,512]{2,1,0:T(8,128)(2,1)} %get-tuple-element.24.v_ref, ...), custom_call_target="tpu_custom_call" | custom-call | flops 14763950080 | bytes 9000000 | tf_op jit(solution)/shard_map/attend_back/pallas_call | solution.py:232
  107.9 4.5 %fusion.5.refs_0_ = f32[4,384,640]{2,1,0:T(8,128)} fusion(bf16[4,384,512]{2,1,0:T(8,128)(2,1)S(1)} %bitcast.172, bf16[1408,512]{1,0:T(8,128)(2,1)} %bitcast.182), kind=kOutput, calls=%fused_computation.15 | convolution fusion | flops 1006632960 | bytes 6160384 | tf_op jit(solution)/shard_map/dot_general | solution.py:27
  112.4 7.1 %collective-permute-done.6.refs_1_ = f32[192,768]{1,0:T(8,128)S(1)} collective-permute-done((f32[192,768]{1,0:T(8,128)S(1)}, f32[192,768]{1,0:T(8,128)S(1)}, u32[]{:S(2)}, u32[]{:S(2)}) %collective-permute-start.6) | collective-permute-done | bytes 589856 | tf_op jit(solution)/shard_map/ppermute | solution.py:373
  124.6 6.9 %all-to-all-start.1 = ((f32[16,88,512]{2,1,0:T(8,128)}), f32[16,88,512]{2,1,0:T(8,128)S(1)}, u32[]{:S(2)}, u32[]{:S(2)}) async-start(f32[16,88,512]{2,1,0:T(8,128)} %bitcast.178), calls=%async_computation.1 | async-start | bytes 5767168 | tf_op jit(solution)/shard_map/all_to_all | solution.py:439
  141.2 3.5 %constant_dynamic-slice_fusion.6 = bf16[1024,704]{1,0:T(8,128)(2,1)} fusion(bf16[1024,1408]{1,0:T(8,128)(2,1)} %latents.1, s32[]{:T(128)S(6)} %select_n.163), kind=kLoop, calls=%fused_computation.107 | loop fusion | bytes 2883588 | tf_op jit(solution)/shard_map/dynamic_slice | solution.py:477
  155.6 15.9 %all-to-all-done.1.pieces_ref = f32[16,88,512]{2,1,0:T(8,128)S(1)} async-done(((f32[16,88,512]{2,1,0:T(8,128)}), f32[16,88,512]{2,1,0:T(8,128)S(1)}, u32[]{:S(2)}, u32[]{:S(2)}) %all-to-all-start.1) | async-done | bytes 2883616 | tf_op jit(solution)/shard_map/all_to_all | solution.py:439
  173.0 4.3 %query_grad.1 = f32[16,88,256]{2,1,0:T(8,128)} custom-call(f32[16,88,512]{2,1,0:T(8,128)} %copy-done.1, bf16[1408,512]{1,0:T(8,128)(2,1)} %constant_dynamic-slice_fusion.2.norm_ref), custom_call_target="tpu_custom_call" | custom-call | flops 126877696 | bytes 6000000 | tf_op jit(solution)/shard_map/query_grad/pallas_call | solution.py:334
  177.3 3.8 %all-to-all-start.2 = ((f32[16,88,256]{2,1,0:T(8,128)}), f32[16,88,256]{2,1,0:T(8,128)S(1)}, u32[]{:S(2)}, u32[]{:S(2)}) async-start(f32[16,88,256]{2,1,0:T(8,128)} %query_grad.1), calls=%async_computation.2 | async-start | bytes 2883584 | tf_op jit(solution)/shard_map/all_to_all | solution.py:464
  198.2 9.5 %all-to-all-done.2.after_ref = f32[16,88,256]{2,1,0:T(8,128)S(1)} async-done(((f32[16,88,256]{2,1,0:T(8,128)}), f32[16,88,256]{2,1,0:T(8,128)S(1)}, u32[]{:S(2)}, u32[]{:S(2)}) %all-to-all-start.2) | async-done | bytes 1441824 | tf_op jit(solution)/shard_map/all_to_all | solution.py:464
  208.8 6.5 %project_out.1 = (f32[88,704]{1,0:T(8,128)}, f32[704,1024]{1,0:T(8,128)}, f32[704,1024]{1,0:T(8,128)}) custom-call(f32[2,8,88,512]{3,2,1,0:T(8,128)} %bitcast.202, bf16[88,1024]{1,0:T(8,128)(2,1)} %bitcast.185, bf16[704,704]{1,0:T(8,128)(2,1)} %bitcast.184, bf16[704,704]{1,0:T(8,128)(2,1)} %bitcast.183, f32[16,88,256]{2,1,0:T(8,128)} %copy-done.4), custom_call_target="tpu_custom_call" | custom-call | flops 2030043136 | bytes 12000000 | tf_op jit(solution)/shard_map/project_out/pallas_call | solution.py:291
  221.1 9.2 %collective-permute-done.24 = f32[4,24,640]{2,1,0:T(8,128)S(1)} collective-permute-done((f32[4,24,640]{2,1,0:T(8,128)S(1)}, f32[4,24,640]{2,1,0:T(8,128)S(1)}, u32[]{:S(2)}, u32[]{:S(2)}) %collective-permute-start.24) | collective-permute-done | bytes 245792 | tf_op jit(solution)/shard_map/ppermute | solution.py:373
  235.1 5.0 %collective-permute-done.16 = f32[4,24,768]{2,1,0:T(8,128)S(1)} collective-permute-done((f32[4,24,768]{2,1,0:T(8,128)S(1)}, f32[4,24,768]{2,1,0:T(8,128)S(1)}, u32[]{:S(2)}, u32[]{:S(2)}) %collective-permute-start.16) | collective-permute-done | bytes 294944 | tf_op jit(solution)/shard_map/ppermute | solution.py:373
  240.2 6.9 %collective-permute-start.27 = (f32[24,640]{1,0:T(8,128)S(1)}, f32[24,640]{1,0:T(8,128)S(1)}, u32[]{:S(2)}, u32[]{:S(2)}) collective-permute-start(f32[24,640]{1,0:T(8,128)S(1)} %get-tuple-element.73), channel_id=1, source_target_pairs={{0,8},{8,16},{16,24},{24,0},{32,40},{40,48},{48,56},{56,32},{64,72... | collective-permute-start | bytes 184328 | tf_op jit(solution)/shard_map/ppermute | solution.py:373
  247.3 3.2 %collective-permute-start.19 = (f32[24,768]{1,0:T(8,128)S(1)}, f32[24,768]{1,0:T(8,128)S(1)}, u32[]{:S(2)}, u32[]{:S(2)}) collective-permute-start(f32[24,768]{1,0:T(8,128)S(1)} %get-tuple-element.65), channel_id=1, source_target_pairs={{0,96},{8,104},{16,112},{24,120},{32,0},{40,8},{48,16},{56,24},{64... | collective-permute-start | bytes 221192 | tf_op jit(solution)/shard_map/ppermute | solution.py:373
  258.0 3.2 %latent_grad.1 = f32[8,64,176]{2,1,0:T(8,128)} custom-call(f32[8,88,64]{2,1,0:T(8,128)} %constant_dynamic-slice_fusion.1.pieces_ref, bf16[704,1408]{1,0:T(8,128)(2,1)} %bitcast.180, bf16[64,1408]{1,0:T(8,128)(2,1)} %constant_dynamic-slice_fusion.latents_ref, bf16[64,1408]{1,0:T(8,128)(2,1)} %dynamic-slice_bitcast_fusion.18.cot_ref), custom_call_target="tpu_custom_call" | custom-call | flops 126877696 | bytes 4000000 | tf_op jit(solution)/shard_map/latent_grad/pallas_call | solution.py:356
  261.2 4.1 %all-to-all-start.3 = ((f32[8,64,176]{2,1,0:T(8,128)}), f32[8,64,176]{2,1,0:T(8,128)S(1)}, u32[]{:S(2)}, u32[]{:S(2)}) async-start(f32[8,64,176]{2,1,0:T(8,128)} %latent_grad.1), calls=%async_computation.3 | async-start | bytes 1048576 | tf_op jit(solution)/shard_map/all_to_all | solution.py:471
  272.0 5.7 %collective-permute-done.9 = f32[22,704]{1,0:T(8,128)S(1)} collective-permute-done((f32[22,704]{1,0:T(8,128)S(1)}, f32[22,704]{1,0:T(8,128)S(1)}, u32[]{:S(2)}, u32[]{:S(2)}) %collective-permute-start.9) | collective-permute-done | bytes 61984 | tf_op jit(solution)/shard_map/ppermute | solution.py:373
  284.9 4.6 %fusion.1 = bf16[1,1024,704]{1,2,0:T(8,128)(2,1)} fusion(f32[704,1024]{1,0:T(8,128)} %get-tuple-element.33, f32[704,1024]{1,0:T(8,128)} %collective-permute-done.8, bf16[1024,704]{0,1:T(8,128)(2,1)S(1)} %copy-done.3), kind=kLoop, calls=%fused_computation.2 | loop fusion | flops 2883584 | bytes 8650752 | tf_op jit(solution)/shard_map/broadcast_in_dim | solution.py:482
  (144 shorter events, 110.3 us)
Async XLA Ops:
  72.1 47.6 %all-to-all-start = ((f32[16,88,512]{2,1,0:T(8,128)}), f32[16,88,512]{2,1,0:T(8,128)S(1)}, u32[]{:S(2)}, u32[]{:S(2)}) async-start(f32[16,88,512]{2,1,0:T(8,128)} %bitcast.22), calls=%async_computation | async-start | bytes 5767168 | tf_op jit(solution)/shard_map/all_to_all | solution.py:435
  75.8 131.9 %all-gather.3.cloned.1.call-start = ((), (), s32[]{:S(2)}) async-start(), calls=%async_computation.4 | async-start | bytes 3063808 | tf_op jit(solution)/shard_map/all_gather | solution.py:473
  104.7 14.8 %collective-permute-start.6 = (f32[192,768]{1,0:T(8,128)S(1)}, f32[192,768]{1,0:T(8,128)S(1)}, u32[]{:S(2)}, u32[]{:S(2)}) collective-permute-start(f32[192,768]{1,0:T(8,128)S(1)} %get-tuple-element.42), channel_id=1, source_target_pairs={{0,1},{1,2},{2,3},{3,0},{4,5},{5,6},{6,7},{7,4},{8,9},{9,10},{10,1... | collective-permute-start | bytes 1769480 | tf_op jit(solution)/shard_map/ppermute | solution.py:373
  106.2 13.4 %collective-permute-start.7 = (f32[192,768]{1,0:T(8,128)S(1)}, f32[192,768]{1,0:T(8,128)}, u32[]{:S(2)}, u32[]{:S(2)}) collective-permute-start(f32[192,768]{1,0:T(8,128)S(1)} %get-tuple-element.43), channel_id=1, source_target_pairs={{0,3},{1,0},{2,1},{3,2},{4,7},{5,4},{6,5},{7,6},{8,11},{9,8},{10,9... | collective-permute-start | bytes 1769480 | tf_op jit(solution)/shard_map/ppermute | solution.py:373
  124.6 46.9 %all-to-all-start.1 = ((f32[16,88,512]{2,1,0:T(8,128)}), f32[16,88,512]{2,1,0:T(8,128)S(1)}, u32[]{:S(2)}, u32[]{:S(2)}) async-start(f32[16,88,512]{2,1,0:T(8,128)} %bitcast.178), calls=%async_computation.1 | async-start | bytes 5767168 | tf_op jit(solution)/shard_map/all_to_all | solution.py:439
  134.3 15.5 %collective-permute-start.20 = (f32[192,640]{1,0:T(8,128)}, f32[192,640]{1,0:T(8,128)}, u32[]{:S(2)}, u32[]{:S(2)}) collective-permute-start(f32[192,640]{1,0:T(8,128)} %get-tuple-element.46), channel_id=1, source_target_pairs={{0,1},{1,2},{2,3},{3,0},{4,5},{5,6},{6,7},{7,4},{8,9},{9,10},{10,1... | collective-permute-start | bytes 1474568 | tf_op jit(solution)/shard_map/ppermute | solution.py:373
  135.2 14.6 %collective-permute-start.22 = (f32[192,640]{1,0:T(8,128)}, f32[192,640]{1,0:T(8,128)}, u32[]{:S(2)}, u32[]{:S(2)}) collective-permute-start(f32[192,640]{1,0:T(8,128)} %get-tuple-element.48), channel_id=1, source_target_pairs={{0,3},{1,0},{2,1},{3,2},{4,7},{5,4},{6,5},{7,6},{8,11},{9,8},{10,9... | collective-permute-start | bytes 1474568 | tf_op jit(solution)/shard_map/ppermute | solution.py:373
  152.6 43.7 %collective-permute-start.23 = (f32[384,640]{1,0:T(8,128)}, f32[384,640]{1,0:T(8,128)}, u32[]{:S(2)}, u32[]{:S(2)}) collective-permute-start(f32[384,640]{1,0:T(8,128)} %pad_maximum_fusion.3), channel_id=1, source_target_pairs={{0,3},{1,0},{2,1},{3,2},{4,7},{5,4},{6,5},{7,6},{8,11},{9,8},{10,9... | collective-permute-start | bytes 2949128 | tf_op jit(solution)/shard_map/ppermute | solution.py:373
  154.6 41.6 %collective-permute-start.21 = (f32[384,640]{1,0:T(8,128)}, f32[384,640]{1,0:T(8,128)}, u32[]{:S(2)}, u32[]{:S(2)}) collective-permute-start(f32[384,640]{1,0:T(8,128)} %pad_maximum_fusion.2), channel_id=1, source_target_pairs={{0,1},{1,2},{2,3},{3,0},{4,5},{5,6},{6,7},{7,4},{8,9},{9,10},{10,1... | collective-permute-start | bytes 2949128 | tf_op jit(solution)/shard_map/ppermute | solution.py:373
  177.3 30.3 %all-to-all-start.2 = ((f32[16,88,256]{2,1,0:T(8,128)}), f32[16,88,256]{2,1,0:T(8,128)S(1)}, u32[]{:S(2)}, u32[]{:S(2)}) async-start(f32[16,88,256]{2,1,0:T(8,128)} %query_grad.1), calls=%async_computation.2 | async-start | bytes 2883584 | tf_op jit(solution)/shard_map/all_to_all | solution.py:464
  184.0 34.7 %collective-permute-start.13 = (f32[384,768]{1,0:T(8,128)}, f32[384,768]{1,0:T(8,128)}, u32[]{:S(2)}, u32[]{:S(2)}) collective-permute-start(f32[384,768]{1,0:T(8,128)} %pad_maximum_fusion.1), channel_id=1, source_target_pairs={{0,3},{1,0},{2,1},{3,2},{4,7},{5,4},{6,5},{7,6},{8,11},{9,8},{10,9... | collective-permute-start | bytes 3538952 | tf_op jit(solution)/shard_map/ppermute | solution.py:373
  186.5 32.1 %collective-permute-start.12 = (f32[384,768]{1,0:T(8,128)}, f32[384,768]{1,0:T(8,128)}, u32[]{:S(2)}, u32[]{:S(2)}) collective-permute-start(f32[384,768]{1,0:T(8,128)} %pad_maximum_fusion), channel_id=1, source_target_pairs={{0,1},{1,2},{2,3},{3,0},{4,5},{5,6},{6,7},{7,4},{8,9},{9,10},{10,1... | collective-permute-start | bytes 3538952 | tf_op jit(solution)/shard_map/ppermute | solution.py:373
  215.3 69.6 %collective-permute-start.8 = (f32[704,1024]{1,0:T(8,128)}, f32[704,1024]{1,0:T(8,128)}, u32[]{:S(2)}, u32[]{:S(2)}) collective-permute-start(f32[704,1024]{1,0:T(8,128)} %get-tuple-element.34), channel_id=1, source_target_pairs={{0,4},{4,0},{1,5},{5,1},{2,6},{6,2},{3,7},{7,3},{8,12},{12,8},{9,1... | collective-permute-start | bytes 8650760 | tf_op jit(solution)/shard_map/ppermute | solution.py:481
  215.4 14.9 %collective-permute-start.24 = (f32[4,24,640]{2,1,0:T(8,128)S(1)}, f32[4,24,640]{2,1,0:T(8,128)S(1)}, u32[]{:S(2)}, u32[]{:S(2)}) collective-permute-start(f32[4,24,640]{2,1,0:T(8,128)S(1)} %get-tuple-element.55), channel_id=1, source_target_pairs={{0,32},{8,40},{16,48},{24,56},{32,64},{40,72},{48,80},{56,88},{64,... | collective-permute-start | bytes 737288 | tf_op jit(solution)/shard_map/ppermute | solution.py:373
  216.5 13.7 %collective-permute-start.26 = (f32[4,24,640]{2,1,0:T(8,128)S(1)}, f32[4,24,640]{2,1,0:T(8,128)S(1)}, u32[]{:S(2)}, u32[]{:S(2)}) collective-permute-start(f32[4,24,640]{2,1,0:T(8,128)S(1)} %get-tuple-element.56), channel_id=1, source_target_pairs={{0,96},{8,104},{16,112},{24,120},{32,0},{40,8},{48,16},{56,24},{64... | collective-permute-start | bytes 737288 | tf_op jit(solution)/shard_map/ppermute | solution.py:373
  218.7 13.6 %collective-permute-start.25 = (f32[4,24,640]{2,1,0:T(8,128)S(1)}, f32[4,24,640]{2,1,0:T(8,128)S(1)}, u32[]{:S(2)}, u32[]{:S(2)}) collective-permute-start(f32[4,24,640]{2,1,0:T(8,128)S(1)} %get-tuple-element.57), channel_id=1, source_target_pairs={{0,64},{8,72},{16,80},{24,88},{32,96},{40,104},{48,112},{56,120},{... | collective-permute-start | bytes 737288 | tf_op jit(solution)/shard_map/ppermute | solution.py:373
  221.0 14.2 %collective-permute-start.14 = (f32[4,24,768]{2,1,0:T(8,128)S(1)}, f32[4,24,768]{2,1,0:T(8,128)S(1)}, u32[]{:S(2)}, u32[]{:S(2)}) collective-permute-start(f32[4,24,768]{2,1,0:T(8,128)S(1)} %get-tuple-element.52), channel_id=1, source_target_pairs={{0,8},{8,16},{16,24},{24,0},{32,40},{40,48},{48,56},{56,32},{64,72... | collective-permute-start | bytes 884744 | tf_op jit(solution)/shard_map/ppermute | solution.py:373
  230.3 16.9 %collective-permute-start.15 = (f32[4,24,768]{2,1,0:T(8,128)S(1)}, f32[4,24,768]{2,1,0:T(8,128)S(1)}, u32[]{:S(2)}, u32[]{:S(2)}) collective-permute-start(f32[4,24,768]{2,1,0:T(8,128)S(1)} %get-tuple-element.54), channel_id=1, source_target_pairs={{0,16},{8,24},{16,0},{24,8},{32,48},{40,56},{48,32},{56,40},{64,80... | collective-permute-start | bytes 884744 | tf_op jit(solution)/shard_map/ppermute | solution.py:373
  232.4 14.9 %collective-permute-start.29 = (f32[24,640]{1,0:T(8,128)S(1)}, f32[24,640]{1,0:T(8,128)S(1)}, u32[]{:S(2)}, u32[]{:S(2)}) collective-permute-start(f32[24,640]{1,0:T(8,128)S(1)} %get-tuple-element.71), channel_id=1, source_target_pairs={{0,24},{8,0},{16,8},{24,16},{32,56},{40,32},{48,40},{56,48},{64,88... | collective-permute-start | bytes 184328 | tf_op jit(solution)/shard_map/ppermute | solution.py:373
  235.1 15.4 %collective-permute-start.28 = (f32[24,640]{1,0:T(8,128)S(1)}, f32[24,640]{1,0:T(8,128)S(1)}, u32[]{:S(2)}, u32[]{:S(2)}) collective-permute-start(f32[24,640]{1,0:T(8,128)S(1)} %get-tuple-element.72), channel_id=1, source_target_pairs={{0,16},{8,24},{16,0},{24,8},{32,48},{40,56},{48,32},{56,40},{64,80... | collective-permute-start | bytes 184328 | tf_op jit(solution)/shard_map/ppermute | solution.py:373
  240.2 10.4 %collective-permute-start.27 = (f32[24,640]{1,0:T(8,128)S(1)}, f32[24,640]{1,0:T(8,128)S(1)}, u32[]{:S(2)}, u32[]{:S(2)}) collective-permute-start(f32[24,640]{1,0:T(8,128)S(1)} %get-tuple-element.73), channel_id=1, source_target_pairs={{0,8},{8,16},{16,24},{24,0},{32,40},{40,48},{48,56},{56,32},{64,72... | collective-permute-start | bytes 184328 | tf_op jit(solution)/shard_map/ppermute | solution.py:373
  261.2 18.8 %all-to-all-start.3 = ((f32[8,64,176]{2,1,0:T(8,128)}), f32[8,64,176]{2,1,0:T(8,128)S(1)}, u32[]{:S(2)}, u32[]{:S(2)}) async-start(f32[8,64,176]{2,1,0:T(8,128)} %latent_grad.1), calls=%async_computation.3 | async-start | bytes 1048576 | tf_op jit(solution)/shard_map/all_to_all | solution.py:471
  265.7 12.1 %collective-permute-start.9 = (f32[22,704]{1,0:T(8,128)S(1)}, f32[22,704]{1,0:T(8,128)S(1)}, u32[]{:S(2)}, u32[]{:S(2)}) collective-permute-start(f32[22,704]{1,0:T(8,128)S(1)} %get-tuple-element.67), channel_id=1, source_target_pairs={{0,1},{1,2},{2,3},{3,0},{4,5},{5,6},{6,7},{7,4},{8,9},{9,10},{10,1... | collective-permute-start | bytes 185864 | tf_op jit(solution)/shard_map/ppermute | solution.py:373
  267.8 10.6 %collective-permute-start.11 = (f32[22,704]{1,0:T(8,128)S(1)}, f32[22,704]{1,0:T(8,128)S(1)}, u32[]{:S(2)}, u32[]{:S(2)}) collective-permute-start(f32[22,704]{1,0:T(8,128)S(1)} %get-tuple-element.68), channel_id=1, source_target_pairs={{0,3},{1,0},{2,1},{3,2},{4,7},{5,4},{6,5},{7,6},{8,11},{9,8},{10,9... | collective-permute-start | bytes 185864 | tf_op jit(solution)/shard_map/ppermute | solution.py:373
  (28 other events, 177.0 us)
Sparse Core Ops, SparseCore 0:
  124.7 79.2 all-gather.2
where the time goes:
time: 298 us; the launch traced here: 296 us
  waiting for transfers between devices  74.6 us (25%)
  Pallas kernels  69.1 us (23%)
  starting transfers between devices  64.8 us (22%)
  local copies, waits for them, and re-layouts  40.6 us (14%)
  other arithmetic  25.6 us (9%)
  between operations  14.6 us (5%)
  matrix products  7.07 us (2%)
    ppermute x32, waiting for transfers between devices, shift(): return lax.ppermute(value, axis, pairs)  49.3 us
    ppermute x32, starting transfers between devices, shift(): return lax.ppermute(value, axis, pairs)  46.2 us
    pallas_call x1, Pallas kernels, forward(): pl.pallas_call(functools.partial(forward_kernel, min(256, count // 2)), g...  22.1 us
    all_to_all x1, waiting for transfers between devices, local(): lax.all_to_all(dq.reshape(seqs, HD, half), 'seq', 0, 0, tiled=True)  15.9 us
    pallas_call x1, Pallas kernels, backward(): pl.pallas_call(functools.partial(backward_kernel, min(256, count // 2)),...  15.4 us
    unnamed x32, local copies, waits for them, and re-layouts  15.3 us
    pallas_call x1, Pallas kernels, project(): pl.pallas_call(project_kernel, in_specs=[anywhere] * len(ins), out_specs=...  14.9 us
    all_to_all x1, waiting for transfers between devices, local(): sent = lax.all_to_all(term, 'seq', 0, 0, tiled=True)  9.48 us
  transfers between devices with their start and end apart: 38, of which 18 were waited for; matrix products, arithmetic and copies ran while one was open for 19% of the time, Pallas kernels for 10%

commit v1 on v0

--- a/solution.py
+++ b/solution.py
@@ -476,7 +476,7 @@
     other = lax.dynamic_slice_in_dim(out_weight, (1 - tp) * inner, inner, 1).T
     latent_cols = lax.dynamic_slice_in_dim(latents, tp * inner, inner, 1).T
     out_rows, keep, away = out_step(
-        attended.reshape(2, heads, HD, half), cot_cols, own, other, sent
+        attended.reshape(2, heads, HD, half), cot_cols, own, other, back
     )
     arrived = lax.ppermute(away, "tp", [(0, 1), (1, 0)])
     resampled = (latent_cols.astype(F32) + (keep + arrived)).astype(BF16).T[None]

time: 298 us -> 300 us (level)
  starting transfers between devices: 64.8 us -> 68.1 us
    ppermute x32, starting transfers between devices: 46.2 us -> 50.2 us  [shift(): return lax.ppermute(value, axis, pairs)]
    unnamed x32 -> x26, local copies, waits for them, and re-layouts: 15.3 us -> 14.9 us
  transfers between devices with their start and end apart: 38 -> 38, of which waited for: 18 -> 21; matrix products, arithmetic and copies ran while one was open for 19% -> 20% of each run, Pallas kernels for 10% -> 10%
where the time goes in v1:
time: 300 us; the launch traced here: 298 us
  waiting for transfers between devices  72.3 us (24%)
  Pallas kernels  69.2 us (23%)
  starting transfers between devices  68.1 us (23%)
  local copies, waits for them, and re-layouts  42.2 us (14%)
  other arithmetic  25 us (8%)
  between operations  14.4 us (5%)
  matrix products  7.02 us (2%)
    ppermute x32, starting transfers between devices, shift(): return lax.ppermute(value, axis, pairs)  50.2 us
    ppermute x32, waiting for transfers between devices, shift(): return lax.ppermute(value, axis, pairs)  48.1 us
    pallas_call x1, Pallas kernels, forward(): pl.pallas_call(functools.partial(forward_kernel, min(256, count // 2)), g...  22.1 us
    pallas_call x1, Pallas kernels, backward(): pl.pallas_call(functools.partial(backward_kernel, min(256, count // 2)),...  15.4 us
    pallas_call x1, Pallas kernels, project(): pl.pallas_call(project_kernel, in_specs=[anywhere] * len(ins), out_specs=...  14.9 us
    unnamed x26, local copies, waits for them, and re-layouts  14.9 us
    all_to_all x1, waiting for transfers between devices, local(): lax.all_to_all(dq.reshape(seqs, HD, half), 'seq', 0, 0, tiled=True)  13.1 us
    all_to_all x1, waiting for transfers between devices, local(): sent = lax.all_to_all(term, 'seq', 0, 0, tiled=True)  11 us
  transfers between devices with their start and end apart: 38, of which 21 were waited for; matrix products, arithmetic and copies ran while one was open for 20% of the time, Pallas kernels for 10%

profile of v1, /device:TPU:0, one launch (start us, length us, event | category | flops | bytes accessed | tf_op | source)
XLA Modules:
  0.0 298.2 jit_solution(859961438932390857)
XLA Ops:
  7.2 14.9 %project.1 = (bf16[1408,512]{1,0:T(8,128)(2,1)}, bf16[1408,1024]{1,0:T(8,128)(2,1)}, bf16[8,88,512]{2,1,0:T(8,128)(2,1)}, bf16[8,88,512]{2,1,0:T(8,128)(2,1)}, b...) custom-call(bf16[512,1408]{1,0:T(8,128)(2,1)} %bitcast.205, bf16[704,1408]{1,0:T(8,128)(2,1)} %bitcast.203, ...), custom_call_target="tpu_custom_call" | custom-call | flops 6090129408 | bytes 24000000 | tf_op jit(solution)/shard_map/project/pallas_call | solution.py:114
  22.1 22.1 %attend.1 = (f32[2,8,88,512]{3,2,1,0:T(8,128)}, f32[3,8,1024]{2,1,0:T(8,128)}) custom-call(bf16[8,88,1024]{2,1,0:T(8,128)(2,1)} %get-tuple-element.22.q_ref, bf16[8,88,512]{2,1,0:T(8,128)(2,1)} %get-tuple-element.23.k_ref, bf16[8,88,512]{2,1,0:T(8,128)(2,1)} %get-tuple-element.24.v_ref, bf16[8,88,1024]{2,1,0:T(8,128)(2,1)} %get-tuple-element.25.u_ref), custom_call_target="tpu_custom_call" | custom-call | flops 5905580032 | bytes 9000000 | tf_op jit(solution)/shard_map/attend/pallas_call | solution.py:179
  56.8 4.1 %collective-permute-start.5 = (f32[3,8,1024]{2,1,0:T(8,128)S(1)}, f32[3,8,1024]{2,1,0:T(8,128)S(1)}, u32[]{:S(2)}, u32[]{:S(2)}) collective-permute-start(f32[3,8,1024]{2,1,0:T(8,128)S(1)} %pad_maximum_fusion.4), channel_id=1, source_target_pairs={{0,96},{8,104},{16,112},{24,120},{32,0},{40,8},{48,16},{56,24},{64... | collective-permute-start | bytes 294920 | tf_op jit(solution)/shard_map/ppermute | solution.py:373
  68.2 3.8 %broadcast_multiply_fusion = f32[2,8,88,512]{3,2,1,0:T(8,128)} fusion(f32[2,8,88,512]{3,2,1,0:T(8,128)} %get-tuple-element.26, f32[2,8,512]{2,1,0:T(8,128)S(1)} %divide_bitcast_fusion), kind=kLoop, calls=%fused_computation.3 | loop fusion | flops 720896 | bytes 5799936 | tf_op jit(solution)/shard_map/mul | solution.py:434
  72.0 3.7 %all-to-all-start = ((f32[16,88,512]{2,1,0:T(8,128)}), f32[16,88,512]{2,1,0:T(8,128)S(1)}, u32[]{:S(2)}, u32[]{:S(2)}) async-start(f32[16,88,512]{2,1,0:T(8,128)} %bitcast.22), calls=%async_computation | async-start | bytes 5767168 | tf_op jit(solution)/shard_map/all_to_all | solution.py:435
  75.9 3.3 %reshape.333 = bf16[16,4,22,512]{3,2,1,0:T(8,128)(2,1)} reshape(bf16[1408,512]{1,0:T(8,128)(2,1)} %get-tuple-element.28) | data formatting | bytes 2883584 | tf_op jit(solution)/shard_map/reshape | solution.py:442
  84.1 15.4 %attend_back.1 = (f32[2,8,88,512]{3,2,1,0:T(8,128)}, bf16[2,8,88,512]{3,2,1,0:T(8,128)(2,1)}, f32[8,128]{1,0:T(8,128)}) custom-call(bf16[8,88,1024]{2,1,0:T(8,128)(2,1)} %get-tuple-element.22.q_ref, bf16[8,88,512]{2,1,0:T(8,128)(2,1)} %get-tuple-element.23.k_ref, bf16[8,88,512]{2,1,0:T(8,128)(2,1)} %get-tuple-element.24.v_ref, ...), custom_call_target="tpu_custom_call" | custom-call | flops 14763950080 | bytes 9000000 | tf_op jit(solution)/shard_map/attend_back/pallas_call | solution.py:232
  107.8 4.5 %fusion.5.refs_0_ = f32[4,384,640]{2,1,0:T(8,128)} fusion(bf16[4,384,512]{2,1,0:T(8,128)(2,1)S(1)} %bitcast.172, bf16[1408,512]{1,0:T(8,128)(2,1)} %bitcast.182), kind=kOutput, calls=%fused_computation.15 | convolution fusion | flops 1006632960 | bytes 6160384 | tf_op jit(solution)/shard_map/dot_general | solution.py:27
  112.3 7.1 %collective-permute-done.6.refs_1_ = f32[192,768]{1,0:T(8,128)S(1)} collective-permute-done((f32[192,768]{1,0:T(8,128)S(1)}, f32[192,768]{1,0:T(8,128)S(1)}, u32[]{:S(2)}, u32[]{:S(2)}) %collective-permute-start.6) | collective-permute-done | bytes 589856 | tf_op jit(solution)/shard_map/ppermute | solution.py:373
  124.4 6.9 %all-to-all-start.1 = ((f32[16,88,512]{2,1,0:T(8,128)}), f32[16,88,512]{2,1,0:T(8,128)S(1)}, u32[]{:S(2)}, u32[]{:S(2)}) async-start(f32[16,88,512]{2,1,0:T(8,128)} %bitcast.178), calls=%async_computation.1 | async-start | bytes 5767168 | tf_op jit(solution)/shard_map/all_to_all | solution.py:439
  131.4 3.4 %constant_dynamic-slice_fusion.6 = bf16[1024,704]{1,0:T(8,128)(2,1)} fusion(bf16[1024,1408]{1,0:T(8,128)(2,1)} %latents.1, s32[]{:T(128)S(6)} %select_n.163), kind=kLoop, calls=%fused_computation.107 | loop fusion | bytes 2883588 | tf_op jit(solution)/shard_map/dynamic_slice | solution.py:477
  147.0 4.1 %constant_dynamic-slice_fusion.3 = (bf16[704,704]{1,0:T(8,128)(2,1)}, bf16[704,704]{1,0:T(8,128)(2,1)}) fusion(bf16[704,1408]{1,0:T(8,128)(2,1)} %ow.1, s32[]{:T(128)S(6)} %select_n.167, s32[]{:T(128)S(6)} %select_n.163), kind=kLoop, calls=%fused_computation.104 | loop fusion | bytes 3964936 | tf_op jit(solution)/shard_map/dynamic_slice | solution.py:476
  158.2 13.1 %all-to-all-done.1.pieces_ref = f32[16,88,512]{2,1,0:T(8,128)S(1)} async-done(((f32[16,88,512]{2,1,0:T(8,128)}), f32[16,88,512]{2,1,0:T(8,128)S(1)}, u32[]{:S(2)}, u32[]{:S(2)}) %all-to-all-start.1) | async-done | bytes 2883616 | tf_op jit(solution)/shard_map/all_to_all | solution.py:439
  172.9 4.3 %query_grad.1 = f32[16,88,256]{2,1,0:T(8,128)} custom-call(f32[16,88,512]{2,1,0:T(8,128)} %copy-done.1, bf16[1408,512]{1,0:T(8,128)(2,1)} %constant_dynamic-slice_fusion.2.norm_ref), custom_call_target="tpu_custom_call" | custom-call | flops 126877696 | bytes 6000000 | tf_op jit(solution)/shard_map/query_grad/pallas_call | solution.py:334
  177.1 3.7 %all-to-all-start.2 = ((f32[16,88,256]{2,1,0:T(8,128)}), f32[16,88,256]{2,1,0:T(8,128)S(1)}, u32[]{:S(2)}, u32[]{:S(2)}) async-start(f32[16,88,256]{2,1,0:T(8,128)} %query_grad.1), calls=%async_computation.2 | async-start | bytes 2883584 | tf_op jit(solution)/shard_map/all_to_all | solution.py:464
  196.4 11.0 %all-to-all-done.2 = f32[16,88,256]{2,1,0:T(8,128)S(1)} async-done(((f32[16,88,256]{2,1,0:T(8,128)}), f32[16,88,256]{2,1,0:T(8,128)S(1)}, u32[]{:S(2)}, u32[]{:S(2)}) %all-to-all-start.2) | async-done | bytes 1441824 | tf_op jit(solution)/shard_map/all_to_all | solution.py:464
  208.2 3.3 %latent_grad.1.after_ref = f32[8,64,176]{2,1,0:T(8,128)} custom-call(f32[8,88,64]{2,1,0:T(8,128)} %constant_dynamic-slice_fusion.1.pieces_ref, bf16[704,1408]{1,0:T(8,128)(2,1)} %bitcast.180, bf16[64,1408]{1,0:T(8,128)(2,1)} %constant_dynamic-slice_fusion.latents_ref, bf16[64,1408]{1,0:T(8,128)(2,1)} %dynamic-slice_bitcast_fusion.18.cot_ref), custom_call_target="tpu_custom_call" | custom-call | flops 126877696 | bytes 4000000 | tf_op jit(solution)/shard_map/latent_grad/pallas_call | solution.py:356
  211.5 6.6 %project_out.1 = (f32[88,704]{1,0:T(8,128)}, f32[704,1024]{1,0:T(8,128)}, f32[704,1024]{1,0:T(8,128)}) custom-call(f32[2,8,88,512]{3,2,1,0:T(8,128)} %bitcast.202, bf16[88,1024]{1,0:T(8,128)(2,1)} %bitcast.185, bf16[704,704]{1,0:T(8,128)(2,1)} %bitcast.184, bf16[704,704]{1,0:T(8,128)(2,1)} %bitcast.183, f32[8,64,176]{2,1,0:T(8,128)} %latent_grad.1.after_ref), custom_call_target="tpu_custom_call" | custom-call | flops 2030043136 | bytes 12000000 | tf_op jit(solution)/shard_map/project_out/pallas_call | solution.py:291
  223.4 8.1 %collective-permute-done.13 = f32[384,768]{1,0:T(8,128)S(1)} collective-permute-done((f32[384,768]{1,0:T(8,128)}, f32[384,768]{1,0:T(8,128)S(1)}, u32[]{:S(2)}, u32[]{:S(2)}) %collective-permute-start.13) | collective-permute-done | bytes 1179680 | tf_op jit(solution)/shard_map/ppermute | solution.py:373
  243.7 4.8 %collective-permute-done.14 = f32[4,24,768]{2,1,0:T(8,128)S(1)} collective-permute-done((f32[4,24,768]{2,1,0:T(8,128)S(1)}, f32[4,24,768]{2,1,0:T(8,128)S(1)}, u32[]{:S(2)}, u32[]{:S(2)}) %collective-permute-start.14) | collective-permute-done | bytes 294944 | tf_op jit(solution)/shard_map/ppermute | solution.py:373
  248.5 3.8 %collective-permute-start.28 = (f32[24,640]{1,0:T(8,128)S(1)}, f32[24,640]{1,0:T(8,128)S(1)}, u32[]{:S(2)}, u32[]{:S(2)}) collective-permute-start(f32[24,640]{1,0:T(8,128)S(1)} %get-tuple-element.72), channel_id=1, source_target_pairs={{0,16},{8,24},{16,0},{24,8},{32,48},{40,56},{48,32},{56,40},{64,80... | collective-permute-start | bytes 184328 | tf_op jit(solution)/shard_map/ppermute | solution.py:373
  263.7 3.5 %all-to-all-start.3 = ((f32[8,64,176]{2,1,0:T(8,128)}), f32[8,64,176]{2,1,0:T(8,128)S(1)}, u32[]{:S(2)}, u32[]{:S(2)}) async-start(f32[8,64,176]{2,1,0:T(8,128)} %latent_grad.1.after_ref), calls=%async_computation.3 | async-start | bytes 1048576 | tf_op jit(solution)/shard_map/all_to_all | solution.py:471
  273.8 5.7 %collective-permute-done.9 = f32[22,704]{1,0:T(8,128)S(1)} collective-permute-done((f32[22,704]{1,0:T(8,128)S(1)}, f32[22,704]{1,0:T(8,128)S(1)}, u32[]{:S(2)}, u32[]{:S(2)}) %collective-permute-start.9) | collective-permute-done | bytes 61984 | tf_op jit(solution)/shard_map/ppermute | solution.py:373
  286.7 4.6 %fusion.1 = bf16[1,1024,704]{1,2,0:T(8,128)(2,1)} fusion(f32[704,1024]{1,0:T(8,128)} %get-tuple-element.33, f32[704,1024]{1,0:T(8,128)} %collective-permute-done.8, bf16[1024,704]{0,1:T(8,128)(2,1)S(1)} %copy-done.3), kind=kLoop, calls=%fused_computation.2 | loop fusion | flops 2883584 | bytes 8650752 | tf_op jit(solution)/shard_map/broadcast_in_dim | solution.py:482
  (138 shorter events, 118.0 us)
Async XLA Ops:
  72.0 47.5 %all-to-all-start = ((f32[16,88,512]{2,1,0:T(8,128)}), f32[16,88,512]{2,1,0:T(8,128)S(1)}, u32[]{:S(2)}, u32[]{:S(2)}) async-start(f32[16,88,512]{2,1,0:T(8,128)} %bitcast.22), calls=%async_computation | async-start | bytes 5767168 | tf_op jit(solution)/shard_map/all_to_all | solution.py:435
  75.8 135.7 %all-gather.3.cloned.1.call-start = ((), (), s32[]{:S(2)}) async-start(), calls=%async_computation.4 | async-start | bytes 3063808 | tf_op jit(solution)/shard_map/all_gather | solution.py:473
  104.6 14.8 %collective-permute-start.6 = (f32[192,768]{1,0:T(8,128)S(1)}, f32[192,768]{1,0:T(8,128)S(1)}, u32[]{:S(2)}, u32[]{:S(2)}) collective-permute-start(f32[192,768]{1,0:T(8,128)S(1)} %get-tuple-element.42), channel_id=1, source_target_pairs={{0,1},{1,2},{2,3},{3,0},{4,5},{5,6},{6,7},{7,4},{8,9},{9,10},{10,1... | collective-permute-start | bytes 1769480 | tf_op jit(solution)/shard_map/ppermute | solution.py:373
  106.2 13.4 %collective-permute-start.7 = (f32[192,768]{1,0:T(8,128)S(1)}, f32[192,768]{1,0:T(8,128)}, u32[]{:S(2)}, u32[]{:S(2)}) collective-permute-start(f32[192,768]{1,0:T(8,128)S(1)} %get-tuple-element.43), channel_id=1, source_target_pairs={{0,3},{1,0},{2,1},{3,2},{4,7},{5,4},{6,5},{7,6},{8,11},{9,8},{10,9... | collective-permute-start | bytes 1769480 | tf_op jit(solution)/shard_map/ppermute | solution.py:373
  124.4 46.9 %all-to-all-start.1 = ((f32[16,88,512]{2,1,0:T(8,128)}), f32[16,88,512]{2,1,0:T(8,128)S(1)}, u32[]{:S(2)}, u32[]{:S(2)}) async-start(f32[16,88,512]{2,1,0:T(8,128)} %bitcast.178), calls=%async_computation.1 | async-start | bytes 5767168 | tf_op jit(solution)/shard_map/all_to_all | solution.py:439
  137.5 43.4 %collective-permute-start.20 = (f32[192,640]{1,0:T(8,128)}, f32[192,640]{1,0:T(8,128)}, u32[]{:S(2)}, u32[]{:S(2)}) collective-permute-start(f32[192,640]{1,0:T(8,128)} %get-tuple-element.46), channel_id=1, source_target_pairs={{0,1},{1,2},{2,3},{3,0},{4,5},{5,6},{6,7},{7,4},{8,9},{9,10},{10,1... | collective-permute-start | bytes 1474568 | tf_op jit(solution)/shard_map/ppermute | solution.py:373
  138.4 42.5 %collective-permute-start.22 = (f32[192,640]{1,0:T(8,128)}, f32[192,640]{1,0:T(8,128)}, u32[]{:S(2)}, u32[]{:S(2)}) collective-permute-start(f32[192,640]{1,0:T(8,128)} %get-tuple-element.48), channel_id=1, source_target_pairs={{0,3},{1,0},{2,1},{3,2},{4,7},{5,4},{6,5},{7,6},{8,11},{9,8},{10,9... | collective-permute-start | bytes 1474568 | tf_op jit(solution)/shard_map/ppermute | solution.py:373
  177.1 30.3 %all-to-all-start.2 = ((f32[16,88,256]{2,1,0:T(8,128)}), f32[16,88,256]{2,1,0:T(8,128)S(1)}, u32[]{:S(2)}, u32[]{:S(2)}) async-start(f32[16,88,256]{2,1,0:T(8,128)} %query_grad.1), calls=%async_computation.2 | async-start | bytes 2883584 | tf_op jit(solution)/shard_map/all_to_all | solution.py:464
  183.6 34.4 %collective-permute-start.23 = (f32[384,640]{1,0:T(8,128)}, f32[384,640]{1,0:T(8,128)}, u32[]{:S(2)}, u32[]{:S(2)}) collective-permute-start(f32[384,640]{1,0:T(8,128)} %pad_maximum_fusion.3), channel_id=1, source_target_pairs={{0,3},{1,0},{2,1},{3,2},{4,7},{5,4},{6,5},{7,6},{8,11},{9,8},{10,9... | collective-permute-start | bytes 2949128 | tf_op jit(solution)/shard_map/ppermute | solution.py:373
  186.1 31.9 %collective-permute-start.21 = (f32[384,640]{1,0:T(8,128)}, f32[384,640]{1,0:T(8,128)}, u32[]{:S(2)}, u32[]{:S(2)}) collective-permute-start(f32[384,640]{1,0:T(8,128)} %pad_maximum_fusion.2), channel_id=1, source_target_pairs={{0,1},{1,2},{2,3},{3,0},{4,5},{5,6},{6,7},{7,4},{8,9},{9,10},{10,1... | collective-permute-start | bytes 2949128 | tf_op jit(solution)/shard_map/ppermute | solution.py:373
  189.4 42.1 %collective-permute-start.13 = (f32[384,768]{1,0:T(8,128)}, f32[384,768]{1,0:T(8,128)S(1)}, u32[]{:S(2)}, u32[]{:S(2)}) collective-permute-start(f32[384,768]{1,0:T(8,128)} %pad_maximum_fusion.1), channel_id=1, source_target_pairs={{0,3},{1,0},{2,1},{3,2},{4,7},{5,4},{6,5},{7,6},{8,11},{9,8},{10,9... | collective-permute-start | bytes 3538952 | tf_op jit(solution)/shard_map/ppermute | solution.py:373
  193.2 42.0 %collective-permute-start.12 = (f32[384,768]{1,0:T(8,128)}, f32[384,768]{1,0:T(8,128)}, u32[]{:S(2)}, u32[]{:S(2)}) collective-permute-start(f32[384,768]{1,0:T(8,128)} %pad_maximum_fusion), channel_id=1, source_target_pairs={{0,1},{1,2},{2,3},{3,0},{4,5},{5,6},{6,7},{7,4},{8,9},{9,10},{10,1... | collective-permute-start | bytes 3538952 | tf_op jit(solution)/shard_map/ppermute | solution.py:373
  218.0 68.6 %collective-permute-start.8 = (f32[704,1024]{1,0:T(8,128)}, f32[704,1024]{1,0:T(8,128)}, u32[]{:S(2)}, u32[]{:S(2)}) collective-permute-start(f32[704,1024]{1,0:T(8,128)} %get-tuple-element.34), channel_id=1, source_target_pairs={{0,4},{4,0},{1,5},{5,1},{2,6},{6,2},{3,7},{7,3},{8,12},{12,8},{9,1... | collective-permute-start | bytes 8650760 | tf_op jit(solution)/shard_map/ppermute | solution.py:481
  220.1 18.8 %collective-permute-start.24 = (f32[4,24,640]{2,1,0:T(8,128)S(1)}, f32[4,24,640]{2,1,0:T(8,128)S(1)}, u32[]{:S(2)}, u32[]{:S(2)}) collective-permute-start(f32[4,24,640]{2,1,0:T(8,128)S(1)} %get-tuple-element.55), channel_id=1, source_target_pairs={{0,32},{8,40},{16,48},{24,56},{32,64},{40,72},{48,80},{56,88},{64,... | collective-permute-start | bytes 737288 | tf_op jit(solution)/shard_map/ppermute | solution.py:373
  220.9 19.6 %collective-permute-start.26 = (f32[4,24,640]{2,1,0:T(8,128)S(1)}, f32[4,24,640]{2,1,0:T(8,128)S(1)}, u32[]{:S(2)}, u32[]{:S(2)}) collective-permute-start(f32[4,24,640]{2,1,0:T(8,128)S(1)} %get-tuple-element.56), channel_id=1, source_target_pairs={{0,96},{8,104},{16,112},{24,120},{32,0},{40,8},{48,16},{56,24},{64... | collective-permute-start | bytes 737288 | tf_op jit(solution)/shard_map/ppermute | solution.py:373
  231.5 10.9 %collective-permute-start.25 = (f32[4,24,640]{2,1,0:T(8,128)S(1)}, f32[4,24,640]{2,1,0:T(8,128)S(1)}, u32[]{:S(2)}, u32[]{:S(2)}) collective-permute-start(f32[4,24,640]{2,1,0:T(8,128)S(1)} %get-tuple-element.57), channel_id=1, source_target_pairs={{0,64},{8,72},{16,80},{24,88},{32,96},{40,104},{48,112},{56,120},{... | collective-permute-start | bytes 737288 | tf_op jit(solution)/shard_map/ppermute | solution.py:373
  237.2 11.4 %collective-permute-start.14 = (f32[4,24,768]{2,1,0:T(8,128)S(1)}, f32[4,24,768]{2,1,0:T(8,128)S(1)}, u32[]{:S(2)}, u32[]{:S(2)}) collective-permute-start(f32[4,24,768]{2,1,0:T(8,128)S(1)} %get-tuple-element.52), channel_id=1, source_target_pairs={{0,8},{8,16},{16,24},{24,0},{32,40},{40,48},{48,56},{56,32},{64,72... | collective-permute-start | bytes 884744 | tf_op jit(solution)/shard_map/ppermute | solution.py:373
  238.9 13.5 %collective-permute-start.16 = (f32[4,24,768]{2,1,0:T(8,128)S(1)}, f32[4,24,768]{2,1,0:T(8,128)S(1)}, u32[]{:S(2)}, u32[]{:S(2)}) collective-permute-start(f32[4,24,768]{2,1,0:T(8,128)S(1)} %get-tuple-element.53), channel_id=1, source_target_pairs={{0,24},{8,0},{16,8},{24,16},{32,56},{40,32},{48,40},{56,48},{64,88... | collective-permute-start | bytes 884744 | tf_op jit(solution)/shard_map/ppermute | solution.py:373
  240.5 13.1 %collective-permute-start.15 = (f32[4,24,768]{2,1,0:T(8,128)S(1)}, f32[4,24,768]{2,1,0:T(8,128)S(1)}, u32[]{:S(2)}, u32[]{:S(2)}) collective-permute-start(f32[4,24,768]{2,1,0:T(8,128)S(1)} %get-tuple-element.54), channel_id=1, source_target_pairs={{0,16},{8,24},{16,0},{24,8},{32,48},{40,56},{48,32},{56,40},{64,80... | collective-permute-start | bytes 884744 | tf_op jit(solution)/shard_map/ppermute | solution.py:373
  242.5 12.8 %collective-permute-start.29 = (f32[24,640]{1,0:T(8,128)S(1)}, f32[24,640]{1,0:T(8,128)S(1)}, u32[]{:S(2)}, u32[]{:S(2)}) collective-permute-start(f32[24,640]{1,0:T(8,128)S(1)} %get-tuple-element.71), channel_id=1, source_target_pairs={{0,24},{8,0},{16,8},{24,16},{32,56},{40,32},{48,40},{56,48},{64,88... | collective-permute-start | bytes 184328 | tf_op jit(solution)/shard_map/ppermute | solution.py:373
  263.7 18.1 %all-to-all-start.3 = ((f32[8,64,176]{2,1,0:T(8,128)}), f32[8,64,176]{2,1,0:T(8,128)S(1)}, u32[]{:S(2)}, u32[]{:S(2)}) async-start(f32[8,64,176]{2,1,0:T(8,128)} %latent_grad.1.after_ref), calls=%async_computation.3 | async-start | bytes 1048576 | tf_op jit(solution)/shard_map/all_to_all | solution.py:471
  267.6 12.0 %collective-permute-start.9 = (f32[22,704]{1,0:T(8,128)S(1)}, f32[22,704]{1,0:T(8,128)S(1)}, u32[]{:S(2)}, u32[]{:S(2)}) collective-permute-start(f32[22,704]{1,0:T(8,128)S(1)} %get-tuple-element.67), channel_id=1, source_target_pairs={{0,1},{1,2},{2,3},{3,0},{4,5},{5,6},{6,7},{7,4},{8,9},{9,10},{10,1... | collective-permute-start | bytes 185864 | tf_op jit(solution)/shard_map/ppermute | solution.py:373
  269.6 10.6 %collective-permute-start.11 = (f32[22,704]{1,0:T(8,128)S(1)}, f32[22,704]{1,0:T(8,128)S(1)}, u32[]{:S(2)}, u32[]{:S(2)}) collective-permute-start(f32[22,704]{1,0:T(8,128)S(1)} %get-tuple-element.68), channel_id=1, source_target_pairs={{0,3},{1,0},{2,1},{3,2},{4,7},{5,4},{6,5},{7,6},{8,11},{9,8},{10,9... | collective-permute-start | bytes 185864 | tf_op jit(solution)/shard_map/ppermute | solution.py:373
  270.9 10.3 %collective-permute-start.10 = (f32[22,704]{1,0:T(8,128)S(1)}, f32[22,704]{1,0:T(8,128)S(1)}, u32[]{:S(2)}, u32[]{:S(2)}) collective-permute-start(f32[22,704]{1,0:T(8,128)S(1)} %get-tuple-element.69), channel_id=1, source_target_pairs={{0,2},{1,3},{2,0},{3,1},{4,6},{5,7},{6,4},{7,5},{8,10},{9,11},{10,... | collective-permute-start | bytes 185864 | tf_op jit(solution)/shard_map/ppermute | solution.py:373
  (25 other events, 141.7 us)
Sparse Core Ops, SparseCore 0:
  124.6 79.2 all-gather.2

commit v2 on v1

--- a/solution.py
+++ b/solution.py
@@ -197,48 +197,46 @@
 def backward_kernel(
     chunk, q_ref, k_ref, v_ref, u_ref, stat_ref, dq_ref, dkv_ref, done_ref
 ):
-    group, _, count = q_ref.shape
+    head = pl.program_id(0)
+    count = q_ref.shape[2]
     half = count // 2
-    for item in range(group):
-        head = pl.program_id(0) * group + item
-        keys_t = k_ref[item]
-        keys = keys_t.astype(F32).T.astype(BF16)
-        vals = v_ref[item].astype(F32).T.astype(BF16)
-        key_grad = jnp.zeros(keys.shape, F32)
-        value_grad = jnp.zeros(vals.shape, F32)
-        total = stat_ref[1, pl.ds(head, 1), :]
-        lse = stat_ref[0, pl.ds(head, 1), :] + jnp.log(total)
-        delta = stat_ref[2, pl.ds(head, 1), :] / total
-        for start in range(0, count, chunk):
-            cols = slice(start, start + chunk)
-            q = q_ref[item, :, cols]
-            u = u_ref[item, :, cols]
-            probs = jnp.exp(dot(keys, q) - lse[:, cols])
-            grad = (probs * (dot(vals, u) - delta[:, cols])).astype(BF16)
-            value_grad += dot(probs.astype(BF16), u.astype(F32).T.astype(BF16))
-            key_grad += dot(grad, q.astype(F32).T.astype(BF16))
-            side, inner = divmod(start, half)
-            dq_ref[side, item, :, inner : inner + chunk] = dot(keys_t, grad)
-        dkv_ref[0, item] = key_grad.T.astype(BF16)
-        dkv_ref[1, item] = value_grad.T.astype(BF16)
+    keys_t = k_ref[0]
+    keys = keys_t.astype(F32).T.astype(BF16)
+    vals = v_ref[0].astype(F32).T.astype(BF16)
+    key_grad = jnp.zeros(keys.shape, F32)
+    value_grad = jnp.zeros(vals.shape, F32)
+    total = stat_ref[1, pl.ds(head, 1), :]
+    lse = stat_ref[0, pl.ds(head, 1), :] + jnp.log(total)
+    delta = stat_ref[2, pl.ds(head, 1), :] / total
+    for start in range(0, count, chunk):
+        cols = slice(start, start + chunk)
+        q = q_ref[0, :, cols]
+        u = u_ref[0, :, cols]
+        probs = jnp.exp(dot(keys, q) - lse[:, cols])
+        grad = (probs * (dot(vals, u) - delta[:, cols])).astype(BF16)
+        value_grad += dot(probs.astype(BF16), u.astype(F32).T.astype(BF16))
+        key_grad += dot(grad, q.astype(F32).T.astype(BF16))
+        side, inner = divmod(start, half)
+        dq_ref[side, 0, :, inner : inner + chunk] = dot(keys_t, grad)
+    dkv_ref[0, 0] = key_grad.T.astype(BF16)
+    dkv_ref[1, 0] = value_grad.T.astype(BF16)
     done_ref[...] = jnp.zeros_like(done_ref)
 
 
 def backward(q, k, v, u, stats):
     heads, _, count = q.shape
     tokens = k.shape[2]
-    group = 1
-    per_head = lambda n: pl.BlockSpec((group, HD, n), lambda h: (h, 0, 0))
+    per_head = lambda n: pl.BlockSpec((1, HD, n), lambda h: (h, 0, 0))
     return pl.pallas_call(
         functools.partial(backward_kernel, min(256, count // 2)),
-        grid=(heads // group,),
+        grid=(heads,),
         in_specs=[
             per_head(count), per_head(tokens), per_head(tokens), per_head(count),
             pl.BlockSpec((3, heads, count), lambda h: (0, 0, 0)),
         ],
         out_specs=[
-            pl.BlockSpec((2, group, HD, count // 2), lambda h: (0, h, 0, 0)),
-            pl.BlockSpec((2, group, HD, tokens), lambda h: (0, h, 0, 0)),
+            pl.BlockSpec((2, 1, HD, count // 2), lambda h: (0, h, 0, 0)),
+            pl.BlockSpec((2, 1, HD, tokens), lambda h: (0, h, 0, 0)),
             pl.BlockSpec((8, 128), lambda h: (0, 0)),
         ],
         out_shape=[
@@ -252,22 +250,21 @@
     )(q, k, v, u, stats)
 
 
-def sum_kernel(pieces_ref, *refs):
-    refs[-1][...] = jnp.sum(pieces_ref[...], 0)
-
-
-def sum_pieces(pieces, *after):
+def sum_kernel(pieces_ref, after_ref, out_ref):
+    out_ref[...] = jnp.sum(pieces_ref[...], 0)
+
+
+def sum_pieces(pieces, after):
     return pl.pallas_call(
         sum_kernel,
-        in_specs=[pl.BlockSpec(memory_space=pltpu.VMEM)] + [pl.BlockSpec(memory_space=pl.ANY)] * len(after),
         out_shape=jax.ShapeDtypeStruct(pieces.shape[1:], F32),
         compiler_params=params(),
         cost_estimate=cost(pieces.size, 4 * pieces.size),
         name="sum_pieces",
-    )(pieces, *after)
-
-
-def out_kernel(att_ref, rows_ref, own_ref, other_ref, after_ref, grad_ref, keep_ref, send_ref):
+    )(pieces, after)
+
+
+def out_kernel(att_ref, rows_ref, own_ref, other_ref, grad_ref, keep_ref, send_ref):
     att = att_ref[0].reshape(own_ref.shape[1], att_ref.shape[3]).astype(BF16)
     term = dot(rows_ref[...], att, NT)
 
@@ -283,7 +280,7 @@
     keep_ref[...] = dot(own_ref[...], att)
 
 
-def out_step(att, rows, own, other, after):
+def out_step(att, rows, own, other):
     _, heads, _, half = att.shape
     width, inner = own.shape
     share = rows.shape[0]
@@ -296,7 +293,6 @@
             pl.BlockSpec((share, half), lambda i: (0, i)),
             whole(own),
             whole(other),
-            pl.BlockSpec(memory_space=pl.ANY),
         ],
         out_specs=[
             pl.BlockSpec((share, inner), lambda i: (0, 0)),
@@ -311,7 +307,7 @@
         compiler_params=params(),
         cost_estimate=cost(8 * half * inner * width, 12e6),
         name="project_out",
-    )(att, rows, own, other, after)
+    )(att, rows, own, other)
 
 
 def query_kernel(pieces_ref, norm_ref, out_ref):
@@ -377,20 +373,18 @@
     return lax.dynamic_index_in_dim(blocks, index, 0, False)
 
 
-def scatter_sum(blocks, axis, place, side=None, minor=True):
+def scatter_sum(blocks, axis, place):
     size = blocks.shape[0]
     total = pick(blocks, place)
     for by in range(1, size):
-        total = total + shift(pick(blocks, (place + by) % size), axis, by, side, minor)
+        total = total + shift(pick(blocks, (place + by) % size), axis, by)
     return total
 
 
-def relay_start(blocks, place, cut, send):
+def relay_sum(blocks, place, cut, send):
     far = pick(blocks, (place + 2) % 4)
-    return send(far[:cut], 1), send(far[cut:], -1)
-
-
-def relay_end(blocks, place, cut, send, front, back):
+    front = send(far[:cut], 1)
+    back = send(far[cut:], -1)
     ahead = pick(blocks, (place + 1) % 4)
     behind = pick(blocks, (place + 3) % 4)
     ahead = jnp.concatenate([ahead[:cut] + front, ahead[cut:]], 0)
@@ -438,50 +432,36 @@
 
     query_pieces = lax.all_to_all(dq.reshape(seqs, HD, half), "seq", 0, 0, tiled=True)
 
-    major, minor = seq // side, seq % side
     blocks = media_norm.reshape(seqs, dps, part, -1).transpose(1, 0, 2, 3)
     blocks = jnp.pad(blocks, ((0, 0), (0, 0), (0, padded - part), (0, 0)))
-    blocks = blocks.reshape(dps * seqs * padded, -1)
-    grads = dkv.reshape(2 * inner, -1)
-    split = (inner // 128 + 1) * 128
-    terms = [dot(blocks, grads[:split], NT), dot(blocks, grads[split:], NT)]
-    terms = [t.reshape(dps, seqs * padded, -1) for t in terms]
-    ring = (dp, seqs * padded // 2, lambda value, by: shift(value, "dp", by))
-    halves = [relay_start(t, *ring) for t in terms]
-    attended = sum_pieces(attended_pieces, terms[1], *halves[0])
-    terms = [relay_end(t, *ring, *h) for t, h in zip(terms, halves)]
-    first, second = (t.reshape(side, side, padded, -1) for t in terms)
-    first = scatter_sum(first.transpose(1, 0, 2, 3), "seq", minor, side, True)
-    first = scatter_sum(first, "seq", major, side, False)
-    second = scatter_sum(second, "seq", major, side, False)
-    second = scatter_sum(second, "seq", minor, side, True)
-    grad_key = first[:part, :inner]
-    grad_value = jnp.concatenate([first[:part, inner:], second[:part]], 1)
-
-    side_of = seq // heads
-    norm_half = lax.dynamic_slice_in_dim(latent_norm, side_of * half, half, 1)
-    term = query_step(query_pieces, norm_half, seqs)
-    sent = lax.all_to_all(term, "seq", 0, 0, tiled=True)
-    strips = lax.dynamic_slice(sent, (side_of * heads, 0, 128), (heads, HD, rows))
-    latent_rows = lax.dynamic_slice_in_dim(latents, seq * rows, rows, 0)
-    cot_rows = lax.dynamic_slice_in_dim(upstream, seq * rows, rows, 0)
-    back = latent_step(strips, query_turned, latent_rows, cot_rows, tps * dps)
-    blocks = (sent[:heads, :, :HD] + sent[heads:, :, :HD]).transpose(1, 0, 2)
-    grad_query = scatter_sum(blocks.reshape(dps, part, inner), "dp", dp)
-    grad_latents = jnp.sum(lax.all_to_all(back, ("tp", "dp"), 0, 0, tiled=True), 0)
-
-    attended = lax.all_gather(attended, "seq")
+    term = dot(blocks.reshape(dps * seqs * padded, -1), dkv.reshape(2 * inner, -1), NT)
+    term = term.reshape(dps, seqs * padded, 2 * inner)
+    term = relay_sum(term, dp, seqs * padded // 2, lambda value, by: shift(value, "dp", by))
+    term = lax.all_to_all(term.reshape(seqs, padded, 2 * inner), "seq", 0, 0, tiled=True)
+    term = jnp.sum(term, 0)[:part]
+    grad_key, grad_value = term[:, :inner], term[:, inner:]
+
+    attended = lax.all_gather(sum_pieces(attended_pieces, done), "seq")
     cot_cols = lax.dynamic_slice_in_dim(upstream, seq * share, share, 1).T
     own = lax.dynamic_slice_in_dim(out_weight, tp * inner, inner, 1).T
     other = lax.dynamic_slice_in_dim(out_weight, (1 - tp) * inner, inner, 1).T
     latent_cols = lax.dynamic_slice_in_dim(latents, tp * inner, inner, 1).T
-    out_rows, keep, away = out_step(
-        attended.reshape(2, heads, HD, half), cot_cols, own, other, back
-    )
+    out_rows, keep, away = out_step(attended.reshape(2, heads, HD, half), cot_cols, own, other)
     arrived = lax.ppermute(away, "tp", [(0, 1), (1, 0)])
     resampled = (latent_cols.astype(F32) + (keep + arrived)).astype(BF16).T[None]
     grad_out = scatter_sum(out_rows.reshape(dps, part, inner), "dp", dp).T
 
+    side_of = seq // heads
+    norm_half = lax.dynamic_slice_in_dim(latent_norm, side_of * half, half, 1)
+    sent = query_step(query_pieces, norm_half, seqs)
+    sent = lax.all_to_all(sent, "seq", 0, 0, tiled=True)
+    strips = lax.dynamic_slice(sent, (side_of * heads, 0, 128), (heads, HD, rows))
+    latent_rows = lax.dynamic_slice_in_dim(latents, seq * rows, rows, 0)
+    cot_rows = lax.dynamic_slice_in_dim(upstream, seq * rows, rows, 0)
+    term = latent_step(strips, query_turned, latent_rows, cot_rows, tps * dps)
+    blocks = (sent[:heads, :, :HD] + sent[heads:, :, :HD]).transpose(1, 0, 2)
+    grad_query = scatter_sum(blocks.reshape(dps, part, inner), "dp", dp)
+    grad_latents = jnp.sum(lax.all_to_all(term, ("tp", "dp"), 0, 0, tiled=True), 0)
     return (resampled, grad_latents, grad_query, grad_key, grad_value, grad_out)
 
 

time: 300 us -> 295 us (0.983)
  waiting for transfers between devices: 72.3 us -> 95.9 us
  starting transfers between devices: 68.1 us -> 51.4 us
  local copies, waits for them, and re-layouts: 42.2 us -> 35.5 us
  matrix products: 7.02 us -> 2.69 us
    all_to_all x1, waiting for transfers between devices: 0.01 us -> 23.6 us  [local(): attended_pieces = lax.all_to_all(scaled, 'seq', 0, 0, tiled=True)]
    ppermute x32 -> x16, starting transfers between devices: 50.2 us -> 26.8 us  [shift(): return lax.ppermute(value, axis, pairs)]
    ppermute x32 -> x16, waiting for transfers between devices: 48.1 us -> 32.7 us  [shift(): return lax.ppermute(value, axis, pairs)]
    all_to_all x2 -> x3, waiting for transfers between devices: 11 us -> 25.8 us  [the longest x1 19.4 us: local(): lax.all_to_all(term.reshape(seqs, padded, 2 * inner), 'seq', 0, 0, tiled=...]
    all_to_all x2 -> x3, starting transfers between devices: 7.2 us -> 16.5 us  [the longest x1 9.1 us: local(): sent = lax.all_to_all(sent, 'seq', 0, 0, tiled=True)]
    dot_general x2 -> x1, matrix products: 7.02 us -> 2.69 us  [dot(): return lax.dot_general(a, b, dims, preferred_element_type=F32)]
    all_to_all x1, starting transfers between devices: 6.89 us -> 3.74 us  [local(): lax.all_to_all(dq.reshape(seqs, HD, half), 'seq', 0, 0, tiled=True)]
    unnamed x26 -> x22, local copies, waits for them, and re-layouts: 14.9 us -> 13.5 us
  transfers between devices with their start and end apart: 38 -> 23, of which waited for: 21 -> 14; matrix products, arithmetic and copies ran while one was open for 20% -> 16% of each run, Pallas kernels for 10% -> 10%
where the time goes in v2:
time: 295 us; the launch traced here: 294 us
  waiting for transfers between devices  95.9 us (33%)
  Pallas kernels  69 us (23%)
  starting transfers between devices  51.4 us (17%)
  local copies, waits for them, and re-layouts  35.5 us (12%)
  other arithmetic  25 us (8%)
  between operations  14.4 us (5%)
    ppermute x16, waiting for transfers between devices, shift(): return lax.ppermute(value, axis, pairs)  32.7 us
    ppermute x16, starting transfers between devices, shift(): return lax.ppermute(value, axis, pairs)  26.8 us
    all_to_all x1, waiting for transfers between devices, local(): attended_pieces = lax.all_to_all(scaled, 'seq', 0, 0, tiled=True)  23.6 us
    pallas_call x1, Pallas kernels, forward(): pl.pallas_call(functools.partial(forward_kernel, min(256, count // 2)), g...  22.1 us
    all_to_all x1, waiting for transfers between devices, local(): lax.all_to_all(term.reshape(seqs, padded, 2 * inner), 'seq', 0, 0, tiled=...  19.4 us
    pallas_call x1, Pallas kernels, backward(): pl.pallas_call(functools.partial(backward_kernel, min(256, count // 2)),...  15.4 us
    pallas_call x1, Pallas kernels, project(): pl.pallas_call(project_kernel, in_specs=[anywhere] * len(ins), out_specs=...  15 us
    all_to_all x1, waiting for transfers between devices, local(): lax.all_to_all(dq.reshape(seqs, HD, half), 'seq', 0, 0, tiled=True)  13.7 us
  transfers between devices with their start and end apart: 23, of which 14 were waited for; matrix products, arithmetic and copies ran while one was open for 16% of the time, Pallas kernels for 10%

profile of v2, /device:TPU:0, one launch (start us, length us, event | category | flops | bytes accessed | tf_op | source)
XLA Modules:
  0.0 294.0 jit_solution(3869425531319526875)
XLA Ops:
  7.2 15.0 %project.1 = (bf16[1408,512]{1,0:T(8,128)(2,1)}, bf16[1408,1024]{1,0:T(8,128)(2,1)}, bf16[8,88,512]{2,1,0:T(8,128)(2,1)}, bf16[8,88,512]{2,1,0:T(8,128)(2,1)}, b...) custom-call(bf16[512,1408]{1,0:T(8,128)(2,1)} %bitcast.128, bf16[704,1408]{1,0:T(8,128)(2,1)} %bitcast.126, ...), custom_call_target="tpu_custom_call" | custom-call | flops 6090129408 | bytes 24000000 | tf_op jit(solution)/shard_map/project/pallas_call | solution.py:114
  22.2 22.1 %attend.1 = (f32[2,8,88,512]{3,2,1,0:T(8,128)}, f32[3,8,1024]{2,1,0:T(8,128)}) custom-call(bf16[8,88,1024]{2,1,0:T(8,128)(2,1)} %get-tuple-element.23.q_ref, bf16[8,88,512]{2,1,0:T(8,128)(2,1)} %get-tuple-element.24.k_ref, bf16[8,88,512]{2,1,0:T(8,128)(2,1)} %get-tuple-element.25.v_ref, bf16[8,88,1024]{2,1,0:T(8,128)(2,1)} %get-tuple-element.26.u_ref), custom_call_target="tpu_custom_call" | custom-call | flops 5905580032 | bytes 9000000 | tf_op jit(solution)/shard_map/attend/pallas_call | solution.py:179
  44.3 2.8 collective-permute-start.2
  56.9 4.1 %collective-permute-start.5 = (f32[3,8,1024]{2,1,0:T(8,128)S(1)}, f32[3,8,1024]{2,1,0:T(8,128)S(1)}, u32[]{:S(2)}, u32[]{:S(2)}) collective-permute-start(f32[3,8,1024]{2,1,0:T(8,128)S(1)} %pad_maximum_fusion.2), channel_id=1, source_target_pairs={{0,96},{8,104},{16,112},{24,120},{32,0},{40,8},{48,16},{56,24},{64... | collective-permute-start | bytes 294920 | tf_op jit(solution)/shard_map/ppermute | solution.py:369
  68.3 3.8 %broadcast_multiply_fusion = f32[2,8,88,512]{3,2,1,0:T(8,128)} fusion(f32[2,8,88,512]{3,2,1,0:T(8,128)} %get-tuple-element.30, f32[2,8,512]{2,1,0:T(8,128)S(1)} %divide_bitcast_fusion), kind=kLoop, calls=%fused_computation.7 | loop fusion | flops 720896 | bytes 5799936 | tf_op jit(solution)/shard_map/mul | solution.py:428
  72.1 3.7 %all-to-all-start = ((f32[16,88,512]{2,1,0:T(8,128)}), f32[16,88,512]{2,1,0:T(8,128)S(1)}, u32[]{:S(2)}, u32[]{:S(2)}) async-start(f32[16,88,512]{2,1,0:T(8,128)} %bitcast.101), calls=%async_computation | async-start | bytes 5767168 | tf_op jit(solution)/shard_map/all_to_all | solution.py:429
  76.7 15.4 %attend_back.1 = (f32[2,8,88,512]{3,2,1,0:T(8,128)}, bf16[2,8,88,512]{3,2,1,0:T(8,128)(2,1)}, f32[8,128]{1,0:T(8,128)}) custom-call(bf16[8,88,1024]{2,1,0:T(8,128)(2,1)} %get-tuple-element.23.q_ref, bf16[8,88,512]{2,1,0:T(8,128)(2,1)} %get-tuple-element.24.k_ref, bf16[8,88,512]{2,1,0:T(8,128)(2,1)} %get-tuple-element.25.v_ref, ...), custom_call_target="tpu_custom_call" | custom-call | flops 14763950080 | bytes 9000000 | tf_op jit(solution)/shard_map/attend_back/pallas_call | solution.py:230
  92.1 23.6 %all-to-all-done.pieces_ref = f32[16,88,512]{2,1,0:T(8,128)S(1)} async-done(((f32[16,88,512]{2,1,0:T(8,128)}), f32[16,88,512]{2,1,0:T(8,128)S(1)}, u32[]{:S(2)}, u32[]{:S(2)}) %all-to-all-start) | async-done | bytes 2883616 | tf_op jit(solution)/shard_map/all_to_all | solution.py:429
  134.5 3.7 %all-to-all-start.1 = ((f32[16,88,512]{2,1,0:T(8,128)}), f32[16,88,512]{2,1,0:T(8,128)S(1)}, u32[]{:S(2)}, u32[]{:S(2)}) async-start(f32[16,88,512]{2,1,0:T(8,128)} %bitcast.103), calls=%async_computation.1 | async-start | bytes 5767168 | tf_op jit(solution)/shard_map/all_to_all | solution.py:433
  138.2 17.5 %collective-permute-done.10 = f32[192,1408]{1,0:T(8,128)} collective-permute-done((f32[192,1408]{1,0:T(8,128)}, f32[192,1408]{1,0:T(8,128)}, u32[]{:S(2)}, u32[]{:S(2)}) %collective-permute-start.10) | collective-permute-done | bytes 1081376 | tf_op jit(solution)/shard_map/ppermute | solution.py:369
  159.7 2.8 collective-permute-start.13
  166.7 13.7 %all-to-all-done.1.pieces_ref = f32[16,88,512]{2,1,0:T(8,128)S(1)} async-done(((f32[16,88,512]{2,1,0:T(8,128)}), f32[16,88,512]{2,1,0:T(8,128)S(1)}, u32[]{:S(2)}, u32[]{:S(2)}) %all-to-all-start.1) | async-done | bytes 2883616 | tf_op jit(solution)/shard_map/all_to_all | solution.py:433
  182.0 4.1 %query_grad.1 = f32[16,88,256]{2,1,0:T(8,128)} custom-call(f32[16,88,512]{2,1,0:T(8,128)} %copy-done, bf16[1408,512]{1,0:T(8,128)(2,1)} %constant_dynamic-slice_fusion.2.norm_ref), custom_call_target="tpu_custom_call" | custom-call | flops 126877696 | bytes 6000000 | tf_op jit(solution)/shard_map/query_grad/pallas_call | solution.py:330
  186.1 9.1 %all-to-all-start.2 = ((f32[16,88,256]{2,1,0:T(8,128)}), f32[16,88,256]{2,1,0:T(8,128)S(1)}, u32[]{:S(2)}, u32[]{:S(2)}) async-start(f32[16,88,256]{2,1,0:T(8,128)} %query_grad.1), calls=%async_computation.2 | async-start | bytes 2883584 | tf_op jit(solution)/shard_map/all_to_all | solution.py:457
  197.2 3.7 %constant_dynamic-slice_fusion.3 = (bf16[704,704]{1,0:T(8,128)(2,1)}, bf16[704,704]{1,0:T(8,128)(2,1)S(1)}) fusion(bf16[704,1408]{1,0:T(8,128)(2,1)} %ow.1, s32[]{:T(128)S(6)} %select_n.75, s32[]{:T(128)S(6)} %select_n.73), kind=kLoop, calls=%fused_computation.62 | loop fusion | bytes 3964936 | tf_op jit(solution)/shard_map/dynamic_slice | solution.py:447
  208.1 6.4 %all-to-all-done.2 = f32[16,88,256]{2,1,0:T(8,128)S(1)} async-done(((f32[16,88,256]{2,1,0:T(8,128)}), f32[16,88,256]{2,1,0:T(8,128)S(1)}, u32[]{:S(2)}, u32[]{:S(2)}) %all-to-all-start.2) | async-done | bytes 1441824 | tf_op jit(solution)/shard_map/all_to_all | solution.py:457
  215.3 3.2 %latent_grad.1 = f32[8,64,176]{2,1,0:T(8,128)} custom-call(f32[8,88,64]{2,1,0:T(8,128)} %constant_dynamic-slice_fusion.1.pieces_ref, bf16[704,1408]{1,0:T(8,128)(2,1)} %bitcast.105, bf16[64,1408]{1,0:T(8,128)(2,1)} %constant_dynamic-slice_fusion.latents_ref, bf16[64,1408]{1,0:T(8,128)(2,1)} %dynamic-slice_bitcast_fusion.6.cot_ref), custom_call_target="tpu_custom_call" | custom-call | flops 126877696 | bytes 4000000 | tf_op jit(solution)/shard_map/latent_grad/pallas_call | solution.py:352
  218.5 3.7 %all-to-all-start.3 = ((f32[8,64,176]{2,1,0:T(8,128)}), f32[8,64,176]{2,1,0:T(8,128)S(1)}, u32[]{:S(2)}, u32[]{:S(2)}) async-start(f32[8,64,176]{2,1,0:T(8,128)} %latent_grad.1), calls=%async_computation.3 | async-start | bytes 1048576 | tf_op jit(solution)/shard_map/all_to_all | solution.py:464
  222.3 6.5 %project_out.1 = (f32[88,704]{1,0:T(8,128)}, f32[704,1024]{1,0:T(8,128)}, f32[704,1024]{1,0:T(8,128)}) custom-call(f32[2,8,88,512]{3,2,1,0:T(8,128)} %bitcast.125, bf16[88,1024]{1,0:T(8,128)(2,1)} %bitcast.109, bf16[704,704]{1,0:T(8,128)(2,1)} %bitcast.108, bf16[704,704]{1,0:T(8,128)(2,1)} %bitcast.107), custom_call_target="tpu_custom_call" | custom-call | flops 2030043136 | bytes 12000000 | tf_op jit(solution)/shard_map/project_out/pallas_call | solution.py:288
  229.2 4.6 %fusion.1 = f32[384,1408]{1,0:T(8,128)} fusion(f32[384,1408]{1,0:T(8,128)} %collective-permute-done.13, f32[384,1408]{1,0:T(8,128)} %collective-permute-done.11, f32[4,384,1408]{2,1,0:T(8,128)} %copy-done.2, s32[]{:T(128)S(6)} %select_n.80), kind=kLoop, calls=%fused_computation.5 | loop fusion | flops 1081344 | bytes 8650756 | tf_op jit(solution)/shard_map/add | solution.py:392
  233.8 3.7 %all-to-all-start.4 = ((f32[16,24,1408]{2,1,0:T(8,128)}), f32[16,24,1408]{2,1,0:T(8,128)S(1)}, u32[]{:S(2)}, u32[]{:S(2)}) async-start(f32[16,24,1408]{2,1,0:T(8,128)} %bitcast.48), calls=%async_computation.4 | async-start | bytes 4325376 | tf_op jit(solution)/shard_map/all_to_all | solution.py:440
  244.8 3.4 %constant_dynamic-slice_fusion.6 = bf16[1024,704]{1,0:T(8,128)(2,1)} fusion(bf16[1024,1408]{1,0:T(8,128)(2,1)} %latents.1, s32[]{:T(128)S(6)} %select_n.73), kind=kLoop, calls=%fused_computation.65 | loop fusion | bytes 2883588 | tf_op jit(solution)/shard_map/dynamic_slice | solution.py:448
  253.0 19.4 %all-to-all-done.4 = f32[16,24,1408]{2,1,0:T(8,128)S(1)} async-done(((f32[16,24,1408]{2,1,0:T(8,128)}), f32[16,24,1408]{2,1,0:T(8,128)S(1)}, u32[]{:S(2)}, u32[]{:S(2)}) %all-to-all-start.4) | async-done | bytes 2162720 | tf_op jit(solution)/shard_map/all_to_all | solution.py:440
  282.5 4.6 %fusion.2 = bf16[1,1024,704]{1,2,0:T(8,128)(2,1)} fusion(f32[704,1024]{1,0:T(8,128)} %get-tuple-element.33, f32[704,1024]{1,0:T(8,128)} %collective-permute-done.6, bf16[1024,704]{0,1:T(8,128)(2,1)S(1)} %copy-done.3), kind=kLoop, calls=%fused_computation.6 | loop fusion | flops 2883584 | bytes 8650752 | tf_op jit(solution)/shard_map/broadcast_in_dim | solution.py:451
  (90 shorter events, 78.8 us)
Async XLA Ops:
  44.3 7.4 %collective-permute-start.2 = (f32[3,8,1024]{2,1,0:T(8,128)}, f32[3,8,1024]{2,1,0:T(8,128)S(1)}, u32[]{:S(2)}, u32[]{:S(2)}) collective-permute-start(f32[3,8,1024]{2,1,0:T(8,128)} %get-tuple-element.27), channel_id=1, source_target_pairs={{0,24},{8,0},{16,8},{24,16},{32,56},{40,32},{48,40},{56,48},{64,88... | collective-permute-start | bytes 294920 | tf_op jit(solution)/shard_map/ppermute | solution.py:369
  47.2 7.1 %collective-permute-start.1 = (f32[3,8,1024]{2,1,0:T(8,128)}, f32[3,8,1024]{2,1,0:T(8,128)S(1)}, u32[]{:S(2)}, u32[]{:S(2)}) collective-permute-start(f32[3,8,1024]{2,1,0:T(8,128)} %get-tuple-element.27), channel_id=1, source_target_pairs={{0,16},{8,24},{16,0},{24,8},{32,48},{40,56},{48,32},{56,40},{64,80... | collective-permute-start | bytes 294920 | tf_op jit(solution)/shard_map/ppermute | solution.py:369
  48.0 7.3 %collective-permute-start = (f32[3,8,1024]{2,1,0:T(8,128)}, f32[3,8,1024]{2,1,0:T(8,128)S(1)}, u32[]{:S(2)}, u32[]{:S(2)}) collective-permute-start(f32[3,8,1024]{2,1,0:T(8,128)} %get-tuple-element.27), channel_id=1, source_target_pairs={{0,8},{8,16},{16,24},{24,0},{32,40},{40,48},{48,56},{56,32},{64,72... | collective-permute-start | bytes 294920 | tf_op jit(solution)/shard_map/ppermute | solution.py:369
  56.9 7.9 %collective-permute-start.5 = (f32[3,8,1024]{2,1,0:T(8,128)S(1)}, f32[3,8,1024]{2,1,0:T(8,128)S(1)}, u32[]{:S(2)}, u32[]{:S(2)}) collective-permute-start(f32[3,8,1024]{2,1,0:T(8,128)S(1)} %pad_maximum_fusion.2), channel_id=1, source_target_pairs={{0,96},{8,104},{16,112},{24,120},{32,0},{40,8},{48,16},{56,24},{64... | collective-permute-start | bytes 294920 | tf_op jit(solution)/shard_map/ppermute | solution.py:369
  61.0 6.5 %collective-permute-start.4 = (f32[3,8,1024]{2,1,0:T(8,128)S(1)}, f32[3,8,1024]{2,1,0:T(8,128)S(1)}, u32[]{:S(2)}, u32[]{:S(2)}) collective-permute-start(f32[3,8,1024]{2,1,0:T(8,128)S(1)} %pad_maximum_fusion.2), channel_id=1, source_target_pairs={{0,64},{8,72},{16,80},{24,88},{32,96},{40,104},{48,112},{56,120},{... | collective-permute-start | bytes 294920 | tf_op jit(solution)/shard_map/ppermute | solution.py:369
  61.0 7.2 %collective-permute-start.3 = (f32[3,8,1024]{2,1,0:T(8,128)S(1)}, f32[3,8,1024]{2,1,0:T(8,128)S(1)}, u32[]{:S(2)}, u32[]{:S(2)}) collective-permute-start(f32[3,8,1024]{2,1,0:T(8,128)S(1)} %pad_maximum_fusion.2), channel_id=1, source_target_pairs={{0,32},{8,40},{16,48},{24,56},{32,64},{40,72},{48,80},{56,88},{64,... | collective-permute-start | bytes 294920 | tf_op jit(solution)/shard_map/ppermute | solution.py:369
  72.1 43.6 %all-to-all-start = ((f32[16,88,512]{2,1,0:T(8,128)}), f32[16,88,512]{2,1,0:T(8,128)S(1)}, u32[]{:S(2)}, u32[]{:S(2)}) async-start(f32[16,88,512]{2,1,0:T(8,128)} %bitcast.101), calls=%async_computation | async-start | bytes 5767168 | tf_op jit(solution)/shard_map/all_to_all | solution.py:429
  75.8 146.5 %all-gather.3.cloned.1.call-start = ((), (), s32[]{:S(2)}) async-start(), calls=%async_computation.5 | async-start | bytes 3063808 | tf_op jit(solution)/shard_map/all_gather | solution.py:444
  131.2 24.4 %collective-permute-start.10 = (f32[192,1408]{1,0:T(8,128)}, f32[192,1408]{1,0:T(8,128)}, u32[]{:S(2)}, u32[]{:S(2)}) collective-permute-start(f32[192,1408]{1,0:T(8,128)} %get-tuple-element.44), channel_id=1, source_target_pairs={{0,1},{1,2},{2,3},{3,0},{4,5},{5,6},{6,7},{7,4},{8,9},{9,10},{10,1... | collective-permute-start | bytes 3244040 | tf_op jit(solution)/shard_map/ppermute | solution.py:369
  132.8 23.0 %collective-permute-start.12 = (f32[192,1408]{1,0:T(8,128)}, f32[192,1408]{1,0:T(8,128)}, u32[]{:S(2)}, u32[]{:S(2)}) collective-permute-start(f32[192,1408]{1,0:T(8,128)} %get-tuple-element.46), channel_id=1, source_target_pairs={{0,3},{1,0},{2,1},{3,2},{4,7},{5,4},{6,5},{7,6},{8,11},{9,8},{10,9... | collective-permute-start | bytes 3244040 | tf_op jit(solution)/shard_map/ppermute | solution.py:369
  134.5 46.0 %all-to-all-start.1 = ((f32[16,88,512]{2,1,0:T(8,128)}), f32[16,88,512]{2,1,0:T(8,128)S(1)}, u32[]{:S(2)}, u32[]{:S(2)}) async-start(f32[16,88,512]{2,1,0:T(8,128)} %bitcast.103), calls=%async_computation.1 | async-start | bytes 5767168 | tf_op jit(solution)/shard_map/all_to_all | solution.py:433
  159.7 69.5 %collective-permute-start.13 = (f32[384,1408]{1,0:T(8,128)}, f32[384,1408]{1,0:T(8,128)}, u32[]{:S(2)}, u32[]{:S(2)}) collective-permute-start(f32[384,1408]{1,0:T(8,128)} %pad_maximum_fusion.1), channel_id=1, source_target_pairs={{0,3},{1,0},{2,1},{3,2},{4,7},{5,4},{6,5},{7,6},{8,11},{9,8},{10,9... | collective-permute-start | bytes 6488072 | tf_op jit(solution)/shard_map/ppermute | solution.py:369
  164.1 65.1 %collective-permute-start.11 = (f32[384,1408]{1,0:T(8,128)}, f32[384,1408]{1,0:T(8,128)}, u32[]{:S(2)}, u32[]{:S(2)}) collective-permute-start(f32[384,1408]{1,0:T(8,128)} %pad_maximum_fusion), channel_id=1, source_target_pairs={{0,1},{1,2},{2,3},{3,0},{4,5},{5,6},{6,7},{7,4},{8,9},{9,10},{10,1... | collective-permute-start | bytes 6488072 | tf_op jit(solution)/shard_map/ppermute | solution.py:369
  186.1 28.4 %all-to-all-start.2 = ((f32[16,88,256]{2,1,0:T(8,128)}), f32[16,88,256]{2,1,0:T(8,128)S(1)}, u32[]{:S(2)}, u32[]{:S(2)}) async-start(f32[16,88,256]{2,1,0:T(8,128)} %query_grad.1), calls=%async_computation.2 | async-start | bytes 2883584 | tf_op jit(solution)/shard_map/all_to_all | solution.py:457
  218.5 15.2 %all-to-all-start.3 = ((f32[8,64,176]{2,1,0:T(8,128)}), f32[8,64,176]{2,1,0:T(8,128)S(1)}, u32[]{:S(2)}, u32[]{:S(2)}) async-start(f32[8,64,176]{2,1,0:T(8,128)} %latent_grad.1), calls=%async_computation.3 | async-start | bytes 1048576 | tf_op jit(solution)/shard_map/all_to_all | solution.py:464
  228.8 53.7 %collective-permute-start.6 = (f32[704,1024]{1,0:T(8,128)}, f32[704,1024]{1,0:T(8,128)}, u32[]{:S(2)}, u32[]{:S(2)}) collective-permute-start(f32[704,1024]{1,0:T(8,128)} %get-tuple-element.34), channel_id=1, source_target_pairs={{0,4},{4,0},{1,5},{5,1},{2,6},{6,2},{3,7},{7,3},{8,12},{12,8},{9,1... | collective-permute-start | bytes 8650760 | tf_op jit(solution)/shard_map/ppermute | solution.py:450
  233.8 38.6 %all-to-all-start.4 = ((f32[16,24,1408]{2,1,0:T(8,128)}), f32[16,24,1408]{2,1,0:T(8,128)S(1)}, u32[]{:S(2)}, u32[]{:S(2)}) async-start(f32[16,24,1408]{2,1,0:T(8,128)} %bitcast.48), calls=%async_computation.4 | async-start | bytes 4325376 | tf_op jit(solution)/shard_map/all_to_all | solution.py:440
  239.6 11.1 %collective-permute-start.7 = (f32[22,704]{1,0:T(8,128)}, f32[22,704]{1,0:T(8,128)S(1)}, u32[]{:S(2)}, u32[]{:S(2)}) collective-permute-start(f32[22,704]{1,0:T(8,128)} %get-tuple-element.56), channel_id=1, source_target_pairs={{0,1},{1,2},{2,3},{3,0},{4,5},{5,6},{6,7},{7,4},{8,9},{9,10},{10,1... | collective-permute-start | bytes 185864 | tf_op jit(solution)/shard_map/ppermute | solution.py:369
  241.3 9.4 %collective-permute-start.9 = (f32[22,704]{1,0:T(8,128)}, f32[22,704]{1,0:T(8,128)S(1)}, u32[]{:S(2)}, u32[]{:S(2)}) collective-permute-start(f32[22,704]{1,0:T(8,128)} %get-tuple-element.57), channel_id=1, source_target_pairs={{0,3},{1,0},{2,1},{3,2},{4,7},{5,4},{6,5},{7,6},{8,11},{9,8},{10,9... | collective-permute-start | bytes 185864 | tf_op jit(solution)/shard_map/ppermute | solution.py:369
  242.8 7.9 %collective-permute-start.8 = (f32[22,704]{1,0:T(8,128)S(1)}, f32[22,704]{1,0:T(8,128)}, u32[]{:S(2)}, u32[]{:S(2)}) collective-permute-start(f32[22,704]{1,0:T(8,128)S(1)} %get-tuple-element.58), channel_id=1, source_target_pairs={{0,2},{1,3},{2,0},{3,1},{4,6},{5,7},{6,4},{7,5},{8,10},{9,11},{10,... | collective-permute-start | bytes 185864 | tf_op jit(solution)/shard_map/ppermute | solution.py:369
  250.7 21.8 %copy-start.7 = (f32[88,704]{1,0:T(8,128)S(1)}, f32[88,704]{1,0:T(8,128)}, u32[]{:S(2)}) copy-start(f32[88,704]{1,0:T(8,128)} %get-tuple-element.39) | copy-start | bytes 743428
  272.6 6.4 %collective-permute-start.14 = (f32[22,704]{1,0:T(8,128)S(1)}, f32[22,704]{1,0:T(8,128)S(1)}, u32[]{:S(2)}, u32[]{:S(2)}) collective-permute-start(f32[22,704]{1,0:T(8,128)S(1)} %get-tuple-element.53), channel_id=1, source_target_pairs={{0,1},{1,2},{2,3},{3,0},{4,5},{5,6},{6,7},{7,4},{8,9},{9,10},{10,1... | collective-permute-start | bytes 185864 | tf_op jit(solution)/shard_map/ppermute | solution.py:369
  274.7 5.1 %collective-permute-start.16 = (f32[22,704]{1,0:T(8,128)S(1)}, f32[22,704]{1,0:T(8,128)S(1)}, u32[]{:S(2)}, u32[]{:S(2)}) collective-permute-start(f32[22,704]{1,0:T(8,128)S(1)} %get-tuple-element.54), channel_id=1, source_target_pairs={{0,3},{1,0},{2,1},{3,2},{4,7},{5,4},{6,5},{7,6},{8,11},{9,8},{10,9... | collective-permute-start | bytes 185864 | tf_op jit(solution)/shard_map/ppermute | solution.py:369
  276.0 5.9 %collective-permute-start.15 = (f32[22,704]{1,0:T(8,128)S(1)}, f32[22,704]{1,0:T(8,128)S(1)}, u32[]{:S(2)}, u32[]{:S(2)}) collective-permute-start(f32[22,704]{1,0:T(8,128)S(1)} %get-tuple-element.55), channel_id=1, source_target_pairs={{0,2},{1,3},{2,0},{3,1},{4,6},{5,7},{6,4},{7,5},{8,10},{9,11},{10,... | collective-permute-start | bytes 185864 | tf_op jit(solution)/shard_map/ppermute | solution.py:369
  (8 other events, 47.7 us)
Sparse Core Ops, SparseCore 0:
  120.0 66.8 all-gather.2
